TPU v7x, 256 devices: a whole 4x4x8 slice. The times are simulated.
256 devices in a mesh: layer: 16 (over z, y_lo), dp: 16 (over x, y_hi, core).
Axes of the slice: x: 4, y: 4 (y_hi: 2, y_lo: 2; y = y_hi * 2 + y_lo), z: 8, core: 2. Of those that a mesh axis runs over, the one named last changes fastest.
Arguments:
- residual: bfloat16 [2, 2048, 3584], P(None, 'dp'), may hold values from -6 to 6
- cotangent: bfloat16 [2, 2048, 3584], P(None, 'dp'), may hold values from -6 to 6
- decoder_first: bfloat16 [8192, 2, 3584], P('layer', None, 'dp'), may hold values from -0.09375 to 0.09375
- decoder_second: bfloat16 [8192, 3584], P('layer', 'dp'), may hold values from -0.09375 to 0.09375
- latent_index: int32 [2, 2048, 64], P(None, 'dp'), may hold values from 0 to 8191, all different within a row
- latent_value: bfloat16 [2, 2048, 64], P(None, 'dp'), may hold values from 0.25 to 3
- active_count: int32 [2, 2048], P(None, 'dp'), may hold values from 8 to 64
Outputs:
- decoder_first_grad: bfloat16 [8192, 2, 3584], P('layer', None, 'dp')
- decoder_second_grad: bfloat16 [8192, 3584], P('layer', 'dp')
- encoder_grad: bfloat16 [3584, 2, 8192], P('dp', None, 'layer')
- latent_grad: float32 [2, 2048, 64], P(None, 'dp')
Inputs may be any that keep to these rules, and one draw needn't show every extreme that they name: `latent_index`: the 64 slots of a token and layer name distinct latents of that layer; slots at or past active_count are padding.
All inputs are finite; a program needn't handle non-finite values.
Results may differ from a plain program's by a relative error of at most 0.02.
Values may be sent and summed in bfloat16 or wider, within the bound.
No kernel may reach another device: no remote copies, remote signals or barrier semaphores. Data moves between devices by JAX's collectives and lax.ppermute only.
A program may use at most 128 MiB of HBM per device.

v0:
```python
import functools
import jax
import jax.numpy as jnp
from jax import lax
from jax.experimental import pallas as pl
from jax.experimental.pallas import tpu as pltpu
from jax.sharding import PartitionSpec as P

BF16 = jnp.bfloat16
F32 = jnp.float32
LANES = 128
RUNS = LANES // 2
SHIFT = 256
EMPTY = 512
STREAM_MIB = 60
KERNEL_MIB = 16
TERMS_MIB = 56
SPOTS_FLOPS = 1 << 32


def grant(mib=KERNEL_MIB):
    return pltpu.CompilerParams(vmem_limit_bytes=mib << 20)


def cost(flops, moved):
    return pl.CostEstimate(flops=flops, bytes_accessed=moved, transcendentals=0)


def lane_pick(table, where):
    return jnp.take_along_axis(table, where, axis=1, mode="promise_in_bounds")


def turn(source, out_ref, base):
    dests = out_ref.shape[0]
    cols = source.shape[1] // dests
    turned = source.T
    for dest in range(dests):
        out_ref[dest, base : base + cols, :] = turned[dest * cols : (dest + 1) * cols]


def kept_slots(own_ref, idx_ref, live_ref, layer, lat_width):
    slots, tokens = idx_ref.shape[1:]
    place = lax.broadcasted_iota(jnp.int32, (slots, tokens), 0)
    local = idx_ref[layer] - own_ref[0]
    inside = (place < live_ref[layer : layer + 1, :]) & (local >= 0) & (local < lat_width)
    return place, local, inside


def pack_kernel(lat_width, own_ref, cot_ref, idx_ref, live_ref, out_ref, rank_ref, slot_ref):
    slots, tokens = idx_ref.shape[1:]
    dests = out_ref.shape[0]
    cols = cot_ref.shape[2] // dests

    @pl.when(pl.program_id(0) == 0)
    def _():
        found = []
        for layer in range(2):
            place, local, inside = kept_slots(own_ref, idx_ref, live_ref, layer, lat_width)
            key = (local & (RUNS - 1)) * 8 + (local >> 6)
            held_key = key - SHIFT
            key = jnp.where(inside, key, 1 << 20)
            rank = jnp.zeros((slots, tokens), jnp.int32)
            for slot in range(slots):
                rank = rank + jnp.where(key[slot : slot + 1, :] < key, 1, 0)
            rank = jnp.where(inside, rank, slots)
            rank_ref[layer] = rank
            held = jnp.full((slots, tokens), EMPTY, jnp.int32)
            for slot in range(slots):
                held = jnp.where(rank[slot : slot + 1, :] == place, held_key[slot : slot + 1, :], held)
            found.append(held.astype(F32))
        slot_ref[...] = jnp.concatenate(found, axis=0).T.astype(BF16)

    for layer in range(2):
        turn(cot_ref[layer], out_ref, layer * cols)
    for dest in range(dests):
        out_ref[dest, 2 * cols :, :] = slot_ref[...]


def pack(lat_width, parts, start, cotangent, index, live):
    _, tokens, width = cotangent.shape
    slots = index.shape[1]
    steps = 4
    rows = 2 * (width // parts) + tokens
    return pl.pallas_call(
        functools.partial(pack_kernel, lat_width),
        grid_spec=pltpu.PrefetchScalarGridSpec(
            num_scalar_prefetch=1,
            grid=(steps,),
            in_specs=[
                pl.BlockSpec((2, tokens, width // steps), lambda i, own: (0, 0, i)),
                pl.BlockSpec((2, slots, tokens), lambda i, own: (0, 0, 0)),
                pl.BlockSpec((2, tokens), lambda i, own: (0, 0)),
            ],
            out_specs=[
                pl.BlockSpec((parts // steps, rows, tokens), lambda i, own: (i, 0, 0)),
                pl.BlockSpec((2, slots, tokens), lambda i, own: (0, 0, 0)),
            ],
            scratch_shapes=[pltpu.VMEM((tokens, LANES), BF16)],
        ),
        out_shape=[
            jax.ShapeDtypeStruct((parts, rows, tokens), BF16),
            jax.ShapeDtypeStruct((2, slots, tokens), jnp.int32),
        ],
        compiler_params=grant(STREAM_MIB),
        cost_estimate=cost(0, 5 << 20),
    )(start, cotangent, index, live)


def half_kernel(own_ref, res_ref, out_ref):
    turn(jnp.concatenate([res_ref[own_ref[1]], res_ref[1 - own_ref[1]]], axis=0), out_ref, 0)


def pack_half(parts, own, residual):
    _, tokens, width = residual.shape
    steps = 4
    share = tokens // 2
    return pl.pallas_call(
        half_kernel,
        grid_spec=pltpu.PrefetchScalarGridSpec(
            num_scalar_prefetch=1,
            grid=(steps,),
            in_specs=[pl.BlockSpec((2, share, width // steps), lambda i, own: (0, own[1], i))],
            out_specs=pl.BlockSpec((parts // steps, width // parts, tokens), lambda i, own: (i, 0, 0)),
        ),
        out_shape=jax.ShapeDtypeStruct((parts, width // parts, tokens), BF16),
        compiler_params=grant(62),
        cost_estimate=cost(0, 2 << 20),
    )(own, residual)


def values_kernel(rank_ref, val_ref, out_ref):
    slots, tokens = val_ref.shape[1:]
    place = lax.broadcasted_iota(jnp.int32, (slots, tokens), 0)
    codes = []
    for layer in range(2):
        rank = rank_ref[layer]
        value = val_ref[layer].astype(F32)
        code = jnp.zeros((slots, tokens), F32)
        for slot in range(slots):
            code = jnp.where(rank[slot : slot + 1, :] == place, value[slot : slot + 1, :], code)
        codes.append(code)
    out_ref[...] = jnp.concatenate(codes, axis=0).T.astype(BF16)


def slot_values(rank, value):
    return pl.pallas_call(
        values_kernel,
        out_shape=jax.ShapeDtypeStruct((value.shape[2], LANES), BF16),
        compiler_params=grant(62),
        cost_estimate=cost(0, 1 << 20),
    )(rank, value)


def terms_kernel(wf_ref, ws_ref, val_ref, half_ref, got_ref, out_ref, weight_ref):
    shards, _, tokens = got_ref.shape
    cols, lat_width = ws_ref.shape

    @pl.when(pl.program_id(0) == 0)
    def _():
        weight_ref[0:cols, 0:lat_width] = wf_ref[0]
        weight_ref[cols : 2 * cols, 0:lat_width] = wf_ref[1]
        weight_ref[0:cols, lat_width:] = jnp.zeros((cols, lat_width), BF16)
        weight_ref[cols : 2 * cols, lat_width:] = ws_ref[...]

    out_ref[:, 2 * tokens :, :] = half_ref[...]
    pair = 2
    for first in range(0, shards, pair):
        some = range(first, first + pair)
        cot = jnp.concatenate([got_ref[shard, 0 : 2 * cols, :] for shard in some], axis=1)
        dense = jnp.dot(cot.T, weight_ref[...], preferred_element_type=F32)
        held = jnp.concatenate([got_ref[shard, 2 * cols :, :] for shard in some], axis=0)
        held = held.astype(F32).astype(jnp.int32) + SHIFT
        lane = lax.broadcasted_iota(jnp.int32, held.shape, 1)
        chunks = lat_width // LANES
        chunk = ((held & 7) >> 1) + jnp.where(lane >= RUNS, chunks, 0)
        chunk = jnp.where(held < lat_width, chunk, 2 * chunks)
        within = jnp.where((held & 1) == 1, RUNS, 0) + (held >> 3)
        picked = jnp.zeros(held.shape, F32)
        for part in range(2 * chunks):
            table = dense[:, part * LANES : (part + 1) * LANES]
            picked = jnp.where(chunk == part, lane_pick(table, within), picked)
        for shard in some:
            out_ref[shard, 0:tokens, :] = picked[(shard - first) * tokens : (shard - first + 1) * tokens].astype(BF16)
            out_ref[shard, tokens : 2 * tokens, :] = val_ref[...]


def slot_terms(first, second, values, half, got):
    parts, rows, tokens = got.shape
    cols, lat_width = second.shape
    shards = 4
    return pl.pallas_call(
        terms_kernel,
        grid=(parts // shards,),
        in_specs=[
            pl.BlockSpec((2, cols, lat_width), lambda i: (0, 0, 0)),
            pl.BlockSpec((cols, lat_width), lambda i: (0, 0)),
            pl.BlockSpec((tokens, LANES), lambda i: (0, 0)),
            pl.BlockSpec((shards, cols, tokens), lambda i: (i, 0, 0)),
            pl.BlockSpec((shards, rows, tokens), lambda i: (i, 0, 0)),
        ],
        out_specs=pl.BlockSpec((shards, 2 * tokens + cols, LANES), lambda i: (i, 0, 0)),
        out_shape=jax.ShapeDtypeStruct((parts, 2 * tokens + cols, LANES), BF16),
        scratch_shapes=[pltpu.VMEM((2 * cols, 2 * lat_width), BF16)],
        compiler_params=grant(TERMS_MIB),
        cost_estimate=cost(2 * parts * tokens * cols * 3 * lat_width, 6 << 20),
    )(first, second, values, half, got)


def total_kernel(got_ref, rank_ref, grad_ref, part_ref):
    total = jnp.sum(got_ref[...].astype(F32), axis=0)
    for dest in range(grad_ref.shape[0]):
        grad_ref[dest] = total.astype(BF16)
    turned = total.T
    slots = rank_ref.shape[1]
    for layer in range(2):
        rank = rank_ref[layer]
        part = jnp.zeros(rank.shape, F32)
        for slot in range(slots):
            row = layer * slots + slot
            part = jnp.where(rank == slot, turned[row : row + 1, :], part)
        part_ref[layer] = part.astype(BF16)


def slot_totals(got, rank):
    parts = got.shape[0]
    tokens = rank.shape[2]
    return pl.pallas_call(
        total_kernel,
        grid=(1,),
        in_specs=[
            pl.BlockSpec((parts, tokens, LANES), lambda i: (0, 0, 0)),
            pl.BlockSpec(rank.shape, lambda i: (0, 0, 0)),
        ],
        out_specs=[
            pl.BlockSpec((parts, tokens, LANES), lambda i: (0, 0, 0)),
            pl.BlockSpec(rank.shape, lambda i: (0, 0, 0)),
        ],
        out_shape=[
            jax.ShapeDtypeStruct((parts, tokens, LANES), BF16),
            jax.ShapeDtypeStruct(rank.shape, BF16),
        ],
        compiler_params=grant(),
        cost_estimate=cost(0, 1 << 20),
    )(got, rank)


FEW = ((8, 4, 2, 1), 3)
ALL = ((32, 16, 8, 4, 2, 1), 8)


def spots_kernel(got_ref, spot_ref):
    shards, _, tokens = got_ref.shape
    top = got_ref.shape[1] - tokens
    lane = lax.broadcasted_iota(jnp.int32, (tokens, LANES), 1)
    place = lane & (RUNS - 1)
    base = lane & RUNS
    last = base + (RUNS - 1)
    start = 8 * place - SHIFT

    def fill(jumps, hops):
        for shard in range(shards):
            held = got_ref[shard, top:, :].astype(F32).astype(jnp.int32)
            below = base
            for jump in jumps:
                further = below + jump
                below = jnp.where(lane_pick(held, further - 1) < start, further, below)
            codes = jnp.zeros((tokens, LANES), jnp.int32)
            for hop in range(hops):
                spot = below if hop == 0 else jnp.minimum(below + hop, last)
                ahead = lane_pick(held, spot) - start
                code = jnp.where((ahead & -8) == 0, ahead + 1, 0)
                if hop > 0:
                    code = jnp.where(below + hop <= last, code, 0)
                codes = codes | jnp.left_shift(code, 4 * hop)
            spot_ref[shard, 0:tokens, :] = below
            spot_ref[shard, tokens:, :] = codes

    deep = jnp.zeros((tokens, LANES), jnp.int32)
    for shard in range(shards):
        held = got_ref[shard, top:, :].astype(F32).astype(jnp.int32)
        ahead = pltpu.roll(held, LANES - FEW[1], 1)
        crowd = ((held >> 3) == (ahead >> 3)) & (place < RUNS - FEW[1])
        many = place == sum(FEW[0])
        deep = jnp.where((held < EMPTY) & (crowd | many), 1, deep)
    deep = jnp.max(deep)

    @pl.when(deep == 0)
    def _():
        fill(*FEW)

    @pl.when(deep != 0)
    def _():
        fill(*ALL)


def slot_spots(got):
    parts, rows, tokens = got.shape
    shards = 2
    return pl.pallas_call(
        spots_kernel,
        grid=(parts // shards,),
        in_specs=[pl.BlockSpec((shards, rows, tokens), lambda i: (i, 0, 0))],
        out_specs=pl.BlockSpec((shards, 2 * tokens, LANES), lambda i: (i, 0, 0)),
        out_shape=jax.ShapeDtypeStruct((parts, 2 * tokens, LANES), jnp.int32),
        compiler_params=grant(56),
        cost_estimate=cost(SPOTS_FLOPS, 8 << 20),
    )(got)


def dense(table, below, codes, hops):
    lane = lax.broadcasted_iota(jnp.int32, below.shape, 1)
    near = lane < RUNS
    far_codes = pltpu.roll(codes, RUNS, 1)
    kept, which = ([], []), ([], [])
    for hop in range(hops):
        spot = below if hop == 0 else jnp.minimum(below + hop, LANES - 1)
        value = lane_pick(table, spot)
        far_value = pltpu.roll(value, RUNS, 1)
        code = (codes >> (4 * hop)) & 15
        far_code = (far_codes >> (4 * hop)) & 15
        kept[0].append(jnp.where(near, value, far_value))
        kept[1].append(jnp.where(near, far_value, value))
        which[0].append(jnp.where(near, code, far_code - 1))
        which[1].append(jnp.where(near, far_code, code - 1))
    for layer in range(2):
        for chunk in range(4):
            found = jnp.zeros(below.shape, F32)
            for hop in range(hops):
                found = jnp.where(which[layer][hop] == 2 * chunk + 1, kept[layer][hop], found)
            yield layer, chunk, found.astype(BF16)


def fill_dense(table_ref, spot_ref, out_ref, halves, product):
    shards, tokens = spot_ref.shape[0], spot_ref.shape[1] // 2
    crowd = jnp.zeros((tokens, LANES), jnp.int32)
    for shard in range(shards):
        crowd = jnp.where((spot_ref[shard, tokens:, :] >> (4 * FEW[1])) != 0, 1, crowd)
    crowd = jnp.max(crowd)

    def fill(hops, shard):
        table = table_ref[shard].astype(F32)
        low = shard * tokens
        if not isinstance(shard, int):
            low = pl.multiple_of(low, tokens)
        for layer, chunk, found in dense(table, spot_ref[shard, 0:tokens, :], spot_ref[shard, tokens:, :], hops):
            at = slice((4 * layer + chunk) * LANES, (4 * layer + chunk + 1) * LANES)
            if halves and layer == 1:
                half = tokens // 2
                found = jnp.concatenate([found[half:], found[:half]], axis=0)
            out_ref[pl.ds(low, tokens), at] = found

    @pl.when(crowd == 0)
    def _():
        for shard in range(shards):
            fill(FEW[1], shard)
            if shard % 2 == 1:
                product(shard - 1)

    @pl.when(crowd != 0)
    def _():
        def one(shard, carry):
            fill(ALL[1], shard)
            return carry

        lax.fori_loop(0, shards, one, 0)
        for shard in range(0, shards, 2):
            product(shard)


def codes_kernel(got_ref, val_ref, spot_ref, first_ref, second_ref, code_ref, sum_ref):
    shards, tokens = spot_ref.shape[0], spot_ref.shape[1] // 2
    cols, lat_width = second_ref.shape
    step = pl.program_id(0)

    @pl.when(step == 0)
    def _():
        sum_ref[...] = jnp.zeros_like(sum_ref)

    def product(first):
        rows = slice(first * tokens, (first + 2) * tokens)
        cot = jnp.concatenate([got_ref[shard, 0 : 2 * cols, :] for shard in (first, first + 1)], axis=1)
        dot = functools.partial(jnp.dot, preferred_element_type=F32)
        sum_ref[0 : 2 * cols, :] += dot(cot, code_ref[rows, 0:lat_width])
        sum_ref[2 * cols : 3 * cols, :] += dot(cot[cols:], code_ref[rows, lat_width:])

    fill_dense(val_ref, spot_ref, code_ref, False, product)

    @pl.when(step == pl.num_programs(0) - 1)
    def _():
        first_ref[0] = sum_ref[0:cols, :].astype(BF16)
        first_ref[1] = sum_ref[cols : 2 * cols, :].astype(BF16)
        second_ref[...] = sum_ref[2 * cols : 3 * cols, :].astype(BF16)


def decoder_grads(got, slots, spots, cols, lat_width):
    parts, rows, tokens = got.shape
    shards = 4
    return pl.pallas_call(
        codes_kernel,
        grid=(parts // shards,),
        in_specs=[
            pl.BlockSpec((shards, rows, tokens), lambda i: (i, 0, 0)),
            pl.BlockSpec((shards, tokens, LANES), lambda i: (i, 1, 0)),
            pl.BlockSpec((shards, 2 * tokens, LANES), lambda i: (i, 0, 0)),
        ],
        out_specs=[
            pl.BlockSpec((2, cols, lat_width), lambda i: (0, 0, 0)),
            pl.BlockSpec((cols, lat_width), lambda i: (0, 0)),
        ],
        out_shape=[
            jax.ShapeDtypeStruct((2, cols, lat_width), BF16),
            jax.ShapeDtypeStruct((cols, lat_width), BF16),
        ],
        scratch_shapes=[
            pltpu.VMEM((shards * tokens, 2 * lat_width), BF16),
            pltpu.VMEM((3 * cols, lat_width), F32),
        ],
        compiler_params=grant(52),
        cost_estimate=cost(2 * parts * tokens * cols * 3 * lat_width, 8 << 20),
    )(got, slots, spots)


def back_kernel(own_ref, mine_ref, other_ref, spot_ref, grad_ref, enc_ref, back_ref, sum_ref):
    shards, tokens = spot_ref.shape[0], spot_ref.shape[1] // 2
    cols, _, lat_width = enc_ref.shape
    step = pl.program_id(0)
    @pl.when(step == 0)
    def _():
        sum_ref[...] = jnp.zeros_like(sum_ref)

    lane = lax.broadcasted_iota(jnp.int32, (cols, tokens), 1)
    mine = (lane < RUNS) == (own_ref[1] == 0)

    def product(first):
        rows = slice(first * tokens, (first + 2) * tokens)
        sides = ([], [])
        for shard in (first, first + 1):
            one, two = mine_ref[shard].astype(F32), other_ref[shard].astype(F32)
            sides[0].append(jnp.where(mine, one, two).astype(BF16))
            sides[1].append(jnp.where(mine, two, one).astype(BF16))
        for layer in range(2):
            sum_ref[layer * cols : (layer + 1) * cols, :] += jnp.dot(
                jnp.concatenate(sides[layer], axis=1),
                back_ref[rows, layer * lat_width : (layer + 1) * lat_width],
                preferred_element_type=F32,
            )

    fill_dense(grad_ref, spot_ref, back_ref, True, product)

    @pl.when(step == pl.num_programs(0) - 1)
    def _():
        enc_ref[:, 0, :] = sum_ref[0:cols, :].astype(BF16)
        enc_ref[:, 1, :] = sum_ref[cols:, :].astype(BF16)


def encoder_grads(own, mine, other, spots, grads, cols, lat_width):
    parts, tokens, _ = grads.shape
    shards = 4
    return pl.pallas_call(
        back_kernel,
        grid=(parts // shards,),
        in_specs=[
            pl.BlockSpec(memory_space=pltpu.SMEM),
            pl.BlockSpec((shards, cols, tokens), lambda i: (i, 0, 0)),
            pl.BlockSpec((shards, cols, tokens), lambda i: (i, 0, 0)),
            pl.BlockSpec((shards,) + spots.shape[1:], lambda i: (i, 0, 0)),
            pl.BlockSpec((shards, tokens, LANES), lambda i: (i, 0, 0)),
        ],
        out_specs=pl.BlockSpec((cols, 2, lat_width), lambda i: (0, 0, 0)),
        out_shape=jax.ShapeDtypeStruct((cols, 2, lat_width), BF16),
        scratch_shapes=[
            pltpu.VMEM((shards * tokens, 2 * lat_width), BF16),
            pltpu.VMEM((2 * cols, lat_width), F32),
        ],
        compiler_params=grant(50),
        cost_estimate=cost(2 * parts * tokens * cols * 2 * lat_width, 8 << 20),
    )(own, mine, other, spots, grads)


def exchange(array, axis):
    return lax.all_to_all(array, axis, 0, 0, tiled=True)


def from_hops(array, axis, size, hops):
    return [lax.ppermute(array, axis, [(at, at ^ hop) for at in range(size)]) for hop in hops]


def shards(layers, parts, residual, cotangent, decoder_first, decoder_second, latent_index, latent_value, active_count):
    lat_width = decoder_first.shape[0]
    cols = decoder_second.shape[1]
    tokens = residual.shape[1]
    members = 2
    place = lax.axis_index("layer")
    own = jnp.stack([place * lat_width, place // 2 % members]).astype(jnp.int32)
    index, value = latent_index.transpose(0, 2, 1), latent_value.transpose(0, 2, 1)
    packed, rank = pack(lat_width, parts, own, cotangent, index, active_count)
    got = exchange(packed, "dp")
    values = slot_values(rank, value)
    half = pack_half(parts, own, residual)
    terms = slot_terms(decoder_first.transpose(1, 2, 0), decoder_second.T, values, half, got)
    slots = exchange(terms, "dp")
    spots = slot_spots(got)
    slots, spots = lax.optimization_barrier((slots, spots))
    grads, part = slot_totals(slots, rank)
    share = slots[:, 2 * tokens :, :]
    (other,) = from_hops(share, "layer", layers, (2,))
    all_grads = exchange(grads, "dp")
    first_grad, second_grad = decoder_grads(got, slots, spots, cols, lat_width)
    part = functools.reduce(jnp.add, from_hops(part, "layer", layers, (1, 2, 3)), part)
    all_grads, first_grad, part = lax.optimization_barrier((all_grads, first_grad, part))
    encoder_grad = encoder_grads(own, share, other, spots, all_grads, cols, lat_width)
    far = from_hops(part, "layer", layers, (4, 8, 12))
    *far, encoder_grad = lax.optimization_barrier((*far, encoder_grad))
    latent_grad = functools.reduce(jnp.add, far, part)
    return (
        first_grad.transpose(2, 0, 1),
        second_grad.T,
        encoder_grad,
        latent_grad.astype(F32).transpose(0, 2, 1),
    )


def solution(mesh):
    return jax.shard_map(
        functools.partial(shards, mesh.shape["layer"], mesh.shape["dp"]),
        mesh=mesh,
        in_specs=(
            P(None, "dp", None),
            P(None, "dp", None),
            P("layer", None, "dp"),
            P("layer", "dp"),
            P(None, "dp", None),
            P(None, "dp", None),
            P(None, "dp"),
        ),
        out_specs=(
            P("layer", None, "dp"),
            P("layer", "dp"),
            P("dp", None, "layer"),
            P(None, "dp", None),
        ),
        check_vma=False,
    )
```

profile of v0, /device:TPU:2, one launch (start us, length us, event | category | flops | bytes accessed | tf_op | source)
XLA Modules:
  0.0 128.5 jit_solution(10523205001352052851)
XLA Ops:
  0.7 0.6 pad_add_fusion.own_ref
  1.2 5.6 %shard_map.102 = (bf16[16,576,128]{2,1,0:T(8,128)(2,1)}, s32[2,64,128]{2,1,0:T(8,128)}) custom-call(s32[2]{0:T(128)} %pad_add_fusion.own_ref, bf16[2,128,3584]{2,1,0:T(8,128)(2,1)} %cot_ref.1, s32[2,64,128]{2,1,0:T(8,128)} %bitcast.12, s32[2,128]{1,0:T(2,128)} %live_ref.1), custom_call_target="tpu_custom_call" | custom-call | bytes 5242880 | tf_op jit(solution)/shard_map/pallas_call | solution.py:84
  6.8 7.5 %all-to-all-start = ((bf16[16,576,128]{2,1,0:T(8,128)(2,1)}), bf16[16,576,128]{2,1,0:T(8,128)(2,1)}, u32[]{:S(2)}, u32[]{:S(2)}) async-start(bf16[16,576,128]{2,1,0:T(8,128)(2,1)} %get-tuple-element.20), calls=%async_computation | async-start | bytes 4718592 | tf_op jit(solution)/shard_map/all_to_all | solution.py:481
  14.3 4.2 %shard_map.104.half_ref = bf16[16,224,128]{2,1,0:T(8,128)(2,1)} custom-call(s32[2]{0:T(128)} %pad_add_fusion.own_ref, bf16[2,128,3584]{2,1,0:T(8,128)(2,1)} %res_ref.1), custom_call_target="tpu_custom_call" | custom-call | bytes 2097152 | tf_op jit(solution)/shard_map/pallas_call | solution.py:117
  18.5 1.8 %shard_map.103.val_ref = bf16[128,128]{1,0:T(8,128)(2,1)} custom-call(s32[2,64,128]{2,1,0:T(8,128)} %get-tuple-element.19.rank_ref, bf16[2,64,128]{2,1,0:T(8,128)(2,1)} %bitcast.13), custom_call_target="tpu_custom_call" | custom-call | bytes 1048576 | tf_op jit(solution)/shard_map/pallas_call | solution.py:146
  20.4 24.5 %all-to-all-done.got_ref = bf16[16,576,128]{2,1,0:T(8,128)(2,1)} async-done(((bf16[16,576,128]{2,1,0:T(8,128)(2,1)}), bf16[16,576,128]{2,1,0:T(8,128)(2,1)}, u32[]{:S(2)}, u32[]{:S(2)}) %all-to-all-start) | async-done | bytes 2359328 | tf_op jit(solution)/shard_map/all_to_all | solution.py:481
  44.9 6.7 %shard_map.105 = bf16[16,480,128]{2,1,0:T(8,128)(2,1)} custom-call(bf16[2,224,512]{2,1,0:T(8,128)(2,1)} %bitcast.10, bf16[224,512]{1,0:T(8,128)(2,1)} %bitcast.11, bf16[128,128]{1,0:T(8,128)(2,1)} %shard_map.103.val_ref, bf16[16,224,128]{2,1,0:T(8,128)(2,1)} %shard_map.104.half_ref, bf16[16,576,128]{2,1,0:T(8,128)(2,1)} %all-to-all-done.got_ref), custom_call_target="tpu_custom_call" | custom-call | flops 1409286144 | bytes 6291456 | tf_op jit(solution)/shard_map/pallas_call | solution.py:191
  51.6 7.2 %all-to-all-start.1 = ((bf16[16,480,128]{2,1,0:T(8,128)(2,1)}), bf16[16,480,128]{2,1,0:T(8,128)(2,1)S(1)}, u32[]{:S(2)}, u32[]{:S(2)}) async-start(bf16[16,480,128]{2,1,0:T(8,128)(2,1)} %shard_map.105), calls=%async_computation.1 | async-start | bytes 3932160 | tf_op jit(solution)/shard_map/all_to_all | solution.py:481
  58.7 10.0 %shard_map.106.spot_ref = s32[16,256,128]{2,1,0:T(8,128)} custom-call(bf16[16,576,128]{2,1,0:T(8,128)(2,1)} %all-to-all-done.got_ref), custom_call_target="tpu_custom_call" | custom-call | flops 4294967296 | bytes 8388608 | tf_op jit(solution)/shard_map/pallas_call | solution.py:299
  68.8 16.2 %all-to-all-done.1.got_ref.val_ref = bf16[16,480,128]{2,1,0:T(8,128)(2,1)S(1)} async-done(((bf16[16,480,128]{2,1,0:T(8,128)(2,1)}), bf16[16,480,128]{2,1,0:T(8,128)(2,1)S(1)}, u32[]{:S(2)}, u32[]{:S(2)}) %all-to-all-start.1) | async-done | bytes 1966112 | tf_op jit(solution)/shard_map/all_to_all | solution.py:481
  85.0 2.0 %collective-permute-start.6 = (bf16[16,224,128]{2,1,0:T(8,128)(2,1)S(1)}, bf16[16,224,128]{2,1,0:T(8,128)(2,1)}, u32[]{:S(2)}, u32[]{:S(2)}) collective-permute-start(bf16[16,224,128]{2,1,0:T(8,128)(2,1)S(1)} %slice.3.mine_ref), channel_id=1, source_target_pairs={{0,32},{16,48},{32,0},{48,16},{64,96},{80,112},{96,64},{112,80},{1... | collective-permute-start | bytes 2752520 | tf_op jit(solution)/shard_map/ppermute | solution.py:485
  87.0 0.5 shard_map.107
  87.5 0.8 copy-done
  88.3 6.2 %all-to-all-start.2 = ((bf16[16,128,128]{2,1,0:T(8,128)(2,1)}), bf16[16,128,128]{2,1,0:T(8,128)(2,1)S(1)}, u32[]{:S(2)}, u32[]{:S(2)}) async-start(bf16[16,128,128]{2,1,0:T(8,128)(2,1)} %copy-done), calls=%async_computation.2 | async-start | bytes 1048576 | tf_op jit(solution)/shard_map/all_to_all | solution.py:481
  94.5 0.3 collective-permute-start.2
  94.8 1.9 %collective-permute-start.1 = (bf16[2,64,128]{2,1,0:T(8,128)(2,1)S(1)}, bf16[2,64,128]{2,1,0:T(8,128)(2,1)S(1)}, u32[]{:S(2)}, u32[]{:S(2)}) collective-permute-start(bf16[2,64,128]{2,1,0:T(8,128)(2,1)S(1)} %get-tuple-element.25), channel_id=1, source_target_pairs={{0,32},{16,48},{32,0},{48,16},{64,96},{80,112},{96,64},{112,80},{1... | collective-permute-start | bytes 98312 | tf_op jit(solution)/shard_map/ppermute | solution.py:485
  96.7 1.3 %collective-permute-start = (bf16[2,64,128]{2,1,0:T(8,128)(2,1)S(1)}, bf16[2,64,128]{2,1,0:T(8,128)(2,1)S(1)}, u32[]{:S(2)}, u32[]{:S(2)}) collective-permute-start(bf16[2,64,128]{2,1,0:T(8,128)(2,1)S(1)} %get-tuple-element.25), channel_id=1, source_target_pairs={{0,16},{16,0},{32,48},{48,32},{64,80},{80,64},{96,112},{112,96},{1... | collective-permute-start | bytes 98312 | tf_op jit(solution)/shard_map/ppermute | solution.py:485
  98.1 10.0 %shard_map.108 = (bf16[2,224,512]{2,1,0:T(8,128)(2,1)}, bf16[224,512]{1,0:T(8,128)(2,1)}) custom-call(bf16[16,576,128]{2,1,0:T(8,128)(2,1)} %all-to-all-done.got_ref, bf16[16,480,128]{2,1,0:T(8,128)(2,1)S(1)} %all-to-all-done.1.got_ref.val_ref, s32[16,256,128]{2,1,0:T(8,128)} %shard_map.106.spot_ref), custom_call_target="tpu_custom_call" | custom-call | flops 1409286144 | bytes 8388608 | tf_op jit(solution)/shard_map/pallas_call | solution.py:398
  108.1 0.2 collective-permute-done.2
  108.6 6.2 %collective-permute-start.5 = (bf16[2,64,128]{2,1,0:T(8,128)(2,1)S(1)}, bf16[2,64,128]{2,1,0:T(8,128)(2,1)S(1)}, u32[]{:S(2)}, u32[]{:S(2)}) collective-permute-start(bf16[2,64,128]{2,1,0:T(8,128)(2,1)S(1)} %add_add_fusion), channel_id=1, source_target_pairs={{0,192},{16,208},{32,224},{48,240},{64,128},{80,144},{96,160},{112... | collective-permute-start | bytes 98312 | tf_op jit(solution)/shard_map/ppermute | solution.py:485
  114.8 1.2 collective-permute-start.4
  116.0 1.5 %collective-permute-start.3 = (bf16[2,64,128]{2,1,0:T(8,128)(2,1)S(1)}, bf16[2,64,128]{2,1,0:T(8,128)(2,1)S(1)}, u32[]{:S(2)}, u32[]{:S(2)}) collective-permute-start(bf16[2,64,128]{2,1,0:T(8,128)(2,1)S(1)} %add_add_fusion), channel_id=1, source_target_pairs={{0,64},{16,80},{32,96},{48,112},{64,0},{80,16},{96,32},{112,48},{1... | collective-permute-start | bytes 98312 | tf_op jit(solution)/shard_map/ppermute | solution.py:485
  117.4 10.4 %shard_map.109 = bf16[224,2,512]{2,1,0:T(2,128)(2,1)} custom-call(s32[2]{0:T(128)S(1)} %copy-done.2, bf16[16,224,128]{2,1,0:T(8,128)(2,1)S(1)} %slice.3.mine_ref, bf16[16,224,128]{2,1,0:T(8,128)(2,1)} %collective-permute-done.6.other_ref, s32[16,256,128]{2,1,0:T(8,128)} %shard_map.106.spot_ref, bf16[16,128,128]{2,1,0:T(8,128)(2,1)S(1)} %all-to-all-done.2.grad_ref), custom_call_target="tpu_custom_call" | custom-call | flops 939524096 | bytes 8388608 | tf_op jit(solution)/shard_map/pallas_call | solution.py:459
  127.9 0.6 convert_bitcast_fusion
  (14 shorter events, 0.3 us)
Async XLA Ops:
  6.8 38.0 %all-to-all-start = ((bf16[16,576,128]{2,1,0:T(8,128)(2,1)}), bf16[16,576,128]{2,1,0:T(8,128)(2,1)}, u32[]{:S(2)}, u32[]{:S(2)}) async-start(bf16[16,576,128]{2,1,0:T(8,128)(2,1)} %get-tuple-element.20), calls=%async_computation | async-start | bytes 4718592 | tf_op jit(solution)/shard_map/all_to_all | solution.py:481
  51.6 33.4 %all-to-all-start.1 = ((bf16[16,480,128]{2,1,0:T(8,128)(2,1)}), bf16[16,480,128]{2,1,0:T(8,128)(2,1)S(1)}, u32[]{:S(2)}, u32[]{:S(2)}) async-start(bf16[16,480,128]{2,1,0:T(8,128)(2,1)} %shard_map.105), calls=%async_computation.1 | async-start | bytes 3932160 | tf_op jit(solution)/shard_map/all_to_all | solution.py:481
  58.7 28.3 %copy-start.1 = (s32[2,64,128]{2,1,0:T(8,128)S(1)}, s32[2,64,128]{2,1,0:T(8,128)}, u32[]{:S(2)}) copy-start(s32[2,64,128]{2,1,0:T(8,128)} %get-tuple-element.19.rank_ref) | copy-start | bytes 196612
  85.0 32.5 %collective-permute-start.6 = (bf16[16,224,128]{2,1,0:T(8,128)(2,1)S(1)}, bf16[16,224,128]{2,1,0:T(8,128)(2,1)}, u32[]{:S(2)}, u32[]{:S(2)}) collective-permute-start(bf16[16,224,128]{2,1,0:T(8,128)(2,1)S(1)} %slice.3.mine_ref), channel_id=1, source_target_pairs={{0,32},{16,48},{32,0},{48,16},{64,96},{80,112},{96,64},{112,80},{1... | collective-permute-start | bytes 2752520 | tf_op jit(solution)/shard_map/ppermute | solution.py:485
  87.5 0.8 copy-start
  88.3 20.3 %all-to-all-start.2 = ((bf16[16,128,128]{2,1,0:T(8,128)(2,1)}), bf16[16,128,128]{2,1,0:T(8,128)(2,1)S(1)}, u32[]{:S(2)}, u32[]{:S(2)}) async-start(bf16[16,128,128]{2,1,0:T(8,128)(2,1)} %copy-done), calls=%async_computation.2 | async-start | bytes 1048576 | tf_op jit(solution)/shard_map/all_to_all | solution.py:481
  94.5 22.9 %copy-start.2 = (s32[2]{0:T(128)S(1)}, s32[2]{0:T(128)}, u32[]{:S(2)}) copy-start(s32[2]{0:T(128)} %pad_add_fusion.own_ref) | copy-start | bytes 28
  94.5 13.8 %collective-permute-start.2 = (bf16[2,64,128]{2,1,0:T(8,128)(2,1)S(1)}, bf16[2,64,128]{2,1,0:T(8,128)(2,1)S(1)}, u32[]{:S(2)}, u32[]{:S(2)}) collective-permute-start(bf16[2,64,128]{2,1,0:T(8,128)(2,1)S(1)} %get-tuple-element.25), channel_id=1, source_target_pairs={{0,48},{16,32},{32,16},{48,0},{64,112},{80,96},{96,80},{112,64},{1... | collective-permute-start | bytes 98312 | tf_op jit(solution)/shard_map/ppermute | solution.py:485
  94.8 13.7 %collective-permute-start.1 = (bf16[2,64,128]{2,1,0:T(8,128)(2,1)S(1)}, bf16[2,64,128]{2,1,0:T(8,128)(2,1)S(1)}, u32[]{:S(2)}, u32[]{:S(2)}) collective-permute-start(bf16[2,64,128]{2,1,0:T(8,128)(2,1)S(1)} %get-tuple-element.25), channel_id=1, source_target_pairs={{0,32},{16,48},{32,0},{48,16},{64,96},{80,112},{96,64},{112,80},{1... | collective-permute-start | bytes 98312 | tf_op jit(solution)/shard_map/ppermute | solution.py:485
  96.7 11.8 %collective-permute-start = (bf16[2,64,128]{2,1,0:T(8,128)(2,1)S(1)}, bf16[2,64,128]{2,1,0:T(8,128)(2,1)S(1)}, u32[]{:S(2)}, u32[]{:S(2)}) collective-permute-start(bf16[2,64,128]{2,1,0:T(8,128)(2,1)S(1)} %get-tuple-element.25), channel_id=1, source_target_pairs={{0,16},{16,0},{32,48},{48,32},{64,80},{80,64},{96,112},{112,96},{1... | collective-permute-start | bytes 98312 | tf_op jit(solution)/shard_map/ppermute | solution.py:485
  108.6 19.3 %collective-permute-start.5 = (bf16[2,64,128]{2,1,0:T(8,128)(2,1)S(1)}, bf16[2,64,128]{2,1,0:T(8,128)(2,1)S(1)}, u32[]{:S(2)}, u32[]{:S(2)}) collective-permute-start(bf16[2,64,128]{2,1,0:T(8,128)(2,1)S(1)} %add_add_fusion), channel_id=1, source_target_pairs={{0,192},{16,208},{32,224},{48,240},{64,128},{80,144},{96,160},{112... | collective-permute-start | bytes 98312 | tf_op jit(solution)/shard_map/ppermute | solution.py:485
  114.8 13.0 %collective-permute-start.4 = (bf16[2,64,128]{2,1,0:T(8,128)(2,1)S(1)}, bf16[2,64,128]{2,1,0:T(8,128)(2,1)S(1)}, u32[]{:S(2)}, u32[]{:S(2)}) collective-permute-start(bf16[2,64,128]{2,1,0:T(8,128)(2,1)S(1)} %add_add_fusion), channel_id=1, source_target_pairs={{0,128},{16,144},{32,160},{48,176},{64,192},{80,208},{96,224},{112... | collective-permute-start | bytes 98312 | tf_op jit(solution)/shard_map/ppermute | solution.py:485
  116.0 11.9 %collective-permute-start.3 = (bf16[2,64,128]{2,1,0:T(8,128)(2,1)S(1)}, bf16[2,64,128]{2,1,0:T(8,128)(2,1)S(1)}, u32[]{:S(2)}, u32[]{:S(2)}) collective-permute-start(bf16[2,64,128]{2,1,0:T(8,128)(2,1)S(1)} %add_add_fusion), channel_id=1, source_target_pairs={{0,64},{16,80},{32,96},{48,112},{64,0},{80,16},{96,32},{112,48},{1... | collective-permute-start | bytes 98312 | tf_op jit(solution)/shard_map/ppermute | solution.py:485
where the time goes:
time: 130 us; the launch traced here: 128 us
  Pallas kernels  49.2 us (38%)
  waiting for transfers between devices  41.2 us (32%)
  starting transfers between devices  35.3 us (27%)
    all_to_all x3, waiting for transfers between devices, exchange(): return lax.all_to_all(array, axis, 0, 0, tiled=True)  40.7 us
    all_to_all x3, starting transfers between devices, exchange(): return lax.all_to_all(array, axis, 0, 0, tiled=True)  20.9 us
    ppermute x7, starting transfers between devices, from_hops(): lax.ppermute(array, axis, [(at, at ^ hop) for at in range(size)])  14.4 us
    pallas_call x1, Pallas kernels, encoder_grads(): pl.pallas_call(back_kernel, grid=(parts // shards,), in_specs=[pl.BlockSp...  10.4 us
    pallas_call x1, Pallas kernels, slot_spots(): pl.pallas_call(spots_kernel, grid=(parts // shards,), in_specs=[pl.BlockS...  10 us
    pallas_call x1, Pallas kernels, decoder_grads(): pl.pallas_call(codes_kernel, grid=(parts // shards,), in_specs=[pl.BlockS...  9.97 us
    pallas_call x1, Pallas kernels, slot_terms(): pl.pallas_call(terms_kernel, grid=(parts // shards,), in_specs=[pl.BlockS...  6.68 us
    pallas_call x1, Pallas kernels, pack(): pl.pallas_call(functools.partial(pack_kernel, lat_width), grid_spec=pltpu...  5.6 us
  transfers between devices with their start and end apart: 10, of which 4 were waited for; matrix products, arithmetic and copies ran while one was open for 0% of the time, Pallas kernels for 29%

commit v1 on v0

--- a/solution.py
+++ b/solution.py
@@ -46,14 +46,14 @@
     return place, local, inside
 
 
-def pack_kernel(lat_width, own_ref, cot_ref, idx_ref, live_ref, out_ref, rank_ref, slot_ref):
+def pack_kernel(lat_width, own_ref, cot_ref, idx_ref, val_ref, live_ref, out_ref, rank_ref, slot_ref):
     slots, tokens = idx_ref.shape[1:]
     dests = out_ref.shape[0]
     cols = cot_ref.shape[2] // dests
 
     @pl.when(pl.program_id(0) == 0)
     def _():
-        found = []
+        found, codes = [], []
         for layer in range(2):
             place, local, inside = kept_slots(own_ref, idx_ref, live_ref, layer, lat_width)
             key = (local & (RUNS - 1)) * 8 + (local >> 6)
@@ -65,10 +65,16 @@
             rank = jnp.where(inside, rank, slots)
             rank_ref[layer] = rank
             held = jnp.full((slots, tokens), EMPTY, jnp.int32)
+            value = val_ref[layer].astype(F32)
+            code = jnp.zeros((slots, tokens), F32)
             for slot in range(slots):
-                held = jnp.where(rank[slot : slot + 1, :] == place, held_key[slot : slot + 1, :], held)
+                here = rank[slot : slot + 1, :] == place
+                held = jnp.where(here, held_key[slot : slot + 1, :], held)
+                code = jnp.where(here, value[slot : slot + 1, :], code)
             found.append(held.astype(F32))
-        slot_ref[...] = jnp.concatenate(found, axis=0).T.astype(BF16)
+            codes.append(code)
+        slot_ref[0:tokens, :] = jnp.concatenate(codes, axis=0).T.astype(BF16)
+        slot_ref[tokens:, :] = jnp.concatenate(found, axis=0).T.astype(BF16)
 
     for layer in range(2):
         turn(cot_ref[layer], out_ref, layer * cols)
@@ -76,11 +82,11 @@
         out_ref[dest, 2 * cols :, :] = slot_ref[...]
 
 
-def pack(lat_width, parts, start, cotangent, index, live):
+def pack(lat_width, parts, start, cotangent, index, value, live):
     _, tokens, width = cotangent.shape
     slots = index.shape[1]
     steps = 4
-    rows = 2 * (width // parts) + tokens
+    rows = 2 * (width // parts) + 2 * tokens
     return pl.pallas_call(
         functools.partial(pack_kernel, lat_width),
         grid_spec=pltpu.PrefetchScalarGridSpec(
@@ -89,13 +95,14 @@
             in_specs=[
                 pl.BlockSpec((2, tokens, width // steps), lambda i, own: (0, 0, i)),
                 pl.BlockSpec((2, slots, tokens), lambda i, own: (0, 0, 0)),
+                pl.BlockSpec((2, slots, tokens), lambda i, own: (0, 0, 0)),
                 pl.BlockSpec((2, tokens), lambda i, own: (0, 0)),
             ],
             out_specs=[
                 pl.BlockSpec((parts // steps, rows, tokens), lambda i, own: (i, 0, 0)),
                 pl.BlockSpec((2, slots, tokens), lambda i, own: (0, 0, 0)),
             ],
-            scratch_shapes=[pltpu.VMEM((tokens, LANES), BF16)],
+            scratch_shapes=[pltpu.VMEM((2 * tokens, LANES), BF16)],
         ),
         out_shape=[
             jax.ShapeDtypeStruct((parts, rows, tokens), BF16),
@@ -103,7 +110,7 @@
         ],
         compiler_params=grant(STREAM_MIB),
         cost_estimate=cost(0, 5 << 20),
-    )(start, cotangent, index, live)
+    )(start, cotangent, index, value, live)
 
 
 def half_kernel(own_ref, res_ref, out_ref):
@@ -128,30 +135,7 @@
     )(own, residual)
 
 
-def values_kernel(rank_ref, val_ref, out_ref):
-    slots, tokens = val_ref.shape[1:]
-    place = lax.broadcasted_iota(jnp.int32, (slots, tokens), 0)
-    codes = []
-    for layer in range(2):
-        rank = rank_ref[layer]
-        value = val_ref[layer].astype(F32)
-        code = jnp.zeros((slots, tokens), F32)
-        for slot in range(slots):
-            code = jnp.where(rank[slot : slot + 1, :] == place, value[slot : slot + 1, :], code)
-        codes.append(code)
-    out_ref[...] = jnp.concatenate(codes, axis=0).T.astype(BF16)
-
-
-def slot_values(rank, value):
-    return pl.pallas_call(
-        values_kernel,
-        out_shape=jax.ShapeDtypeStruct((value.shape[2], LANES), BF16),
-        compiler_params=grant(62),
-        cost_estimate=cost(0, 1 << 20),
-    )(rank, value)
-
-
-def terms_kernel(wf_ref, ws_ref, val_ref, half_ref, got_ref, out_ref, weight_ref):
+def terms_kernel(wf_ref, ws_ref, half_ref, got_ref, out_ref, weight_ref):
     shards, _, tokens = got_ref.shape
     cols, lat_width = ws_ref.shape
 
@@ -162,13 +146,13 @@
         weight_ref[0:cols, lat_width:] = jnp.zeros((cols, lat_width), BF16)
         weight_ref[cols : 2 * cols, lat_width:] = ws_ref[...]
 
-    out_ref[:, 2 * tokens :, :] = half_ref[...]
+    out_ref[:, tokens:, :] = half_ref[...]
     pair = 2
     for first in range(0, shards, pair):
         some = range(first, first + pair)
         cot = jnp.concatenate([got_ref[shard, 0 : 2 * cols, :] for shard in some], axis=1)
         dense = jnp.dot(cot.T, weight_ref[...], preferred_element_type=F32)
-        held = jnp.concatenate([got_ref[shard, 2 * cols :, :] for shard in some], axis=0)
+        held = jnp.concatenate([got_ref[shard, 2 * cols + tokens :, :] for shard in some], axis=0)
         held = held.astype(F32).astype(jnp.int32) + SHIFT
         lane = lax.broadcasted_iota(jnp.int32, held.shape, 1)
         chunks = lat_width // LANES
@@ -181,10 +165,9 @@
             picked = jnp.where(chunk == part, lane_pick(table, within), picked)
         for shard in some:
             out_ref[shard, 0:tokens, :] = picked[(shard - first) * tokens : (shard - first + 1) * tokens].astype(BF16)
-            out_ref[shard, tokens : 2 * tokens, :] = val_ref[...]
-
-
-def slot_terms(first, second, values, half, got):
+
+
+def slot_terms(first, second, half, got):
     parts, rows, tokens = got.shape
     cols, lat_width = second.shape
     shards = 4
@@ -194,16 +177,15 @@
         in_specs=[
             pl.BlockSpec((2, cols, lat_width), lambda i: (0, 0, 0)),
             pl.BlockSpec((cols, lat_width), lambda i: (0, 0)),
-            pl.BlockSpec((tokens, LANES), lambda i: (0, 0)),
             pl.BlockSpec((shards, cols, tokens), lambda i: (i, 0, 0)),
             pl.BlockSpec((shards, rows, tokens), lambda i: (i, 0, 0)),
         ],
-        out_specs=pl.BlockSpec((shards, 2 * tokens + cols, LANES), lambda i: (i, 0, 0)),
-        out_shape=jax.ShapeDtypeStruct((parts, 2 * tokens + cols, LANES), BF16),
+        out_specs=pl.BlockSpec((shards, tokens + cols, LANES), lambda i: (i, 0, 0)),
+        out_shape=jax.ShapeDtypeStruct((parts, tokens + cols, LANES), BF16),
         scratch_shapes=[pltpu.VMEM((2 * cols, 2 * lat_width), BF16)],
         compiler_params=grant(TERMS_MIB),
         cost_estimate=cost(2 * parts * tokens * cols * 3 * lat_width, 6 << 20),
-    )(first, second, values, half, got)
+    )(first, second, half, got)
 
 
 def total_kernel(got_ref, rank_ref, grad_ref, part_ref):
@@ -330,7 +312,7 @@
             yield layer, chunk, found.astype(BF16)
 
 
-def fill_dense(table_ref, spot_ref, out_ref, halves, product):
+def fill_dense(table_ref, top, spot_ref, out_ref, halves, product):
     shards, tokens = spot_ref.shape[0], spot_ref.shape[1] // 2
     crowd = jnp.zeros((tokens, LANES), jnp.int32)
     for shard in range(shards):
@@ -338,7 +320,7 @@
     crowd = jnp.max(crowd)
 
     def fill(hops, shard):
-        table = table_ref[shard].astype(F32)
+        table = table_ref[shard, top : top + tokens, :].astype(F32)
         low = shard * tokens
         if not isinstance(shard, int):
             low = pl.multiple_of(low, tokens)
@@ -367,7 +349,7 @@
             product(shard)
 
 
-def codes_kernel(got_ref, val_ref, spot_ref, first_ref, second_ref, code_ref, sum_ref):
+def codes_kernel(got_ref, spot_ref, first_ref, second_ref, code_ref, sum_ref):
     shards, tokens = spot_ref.shape[0], spot_ref.shape[1] // 2
     cols, lat_width = second_ref.shape
     step = pl.program_id(0)
@@ -383,7 +365,7 @@
         sum_ref[0 : 2 * cols, :] += dot(cot, code_ref[rows, 0:lat_width])
         sum_ref[2 * cols : 3 * cols, :] += dot(cot[cols:], code_ref[rows, lat_width:])
 
-    fill_dense(val_ref, spot_ref, code_ref, False, product)
+    fill_dense(got_ref, 2 * cols, spot_ref, code_ref, False, product)
 
     @pl.when(step == pl.num_programs(0) - 1)
     def _():
@@ -392,7 +374,7 @@
         second_ref[...] = sum_ref[2 * cols : 3 * cols, :].astype(BF16)
 
 
-def decoder_grads(got, slots, spots, cols, lat_width):
+def decoder_grads(got, spots, cols, lat_width):
     parts, rows, tokens = got.shape
     shards = 4
     return pl.pallas_call(
@@ -400,7 +382,6 @@
         grid=(parts // shards,),
         in_specs=[
             pl.BlockSpec((shards, rows, tokens), lambda i: (i, 0, 0)),
-            pl.BlockSpec((shards, tokens, LANES), lambda i: (i, 1, 0)),
             pl.BlockSpec((shards, 2 * tokens, LANES), lambda i: (i, 0, 0)),
         ],
         out_specs=[
@@ -417,7 +398,7 @@
         ],
         compiler_params=grant(52),
         cost_estimate=cost(2 * parts * tokens * cols * 3 * lat_width, 8 << 20),
-    )(got, slots, spots)
+    )(got, spots)
 
 
 def back_kernel(own_ref, mine_ref, other_ref, spot_ref, grad_ref, enc_ref, back_ref, sum_ref):
@@ -445,7 +426,7 @@
                 preferred_element_type=F32,
             )
 
-    fill_dense(grad_ref, spot_ref, back_ref, True, product)
+    fill_dense(grad_ref, 0, spot_ref, back_ref, True, product)
 
     @pl.when(step == pl.num_programs(0) - 1)
     def _():
@@ -493,25 +474,23 @@
     place = lax.axis_index("layer")
     own = jnp.stack([place * lat_width, place // 2 % members]).astype(jnp.int32)
     index, value = latent_index.transpose(0, 2, 1), latent_value.transpose(0, 2, 1)
-    packed, rank = pack(lat_width, parts, own, cotangent, index, active_count)
+    packed, rank = pack(lat_width, parts, own, cotangent, index, value, active_count)
     got = exchange(packed, "dp")
-    values = slot_values(rank, value)
     half = pack_half(parts, own, residual)
-    terms = slot_terms(decoder_first.transpose(1, 2, 0), decoder_second.T, values, half, got)
+    terms = slot_terms(decoder_first.transpose(1, 2, 0), decoder_second.T, half, got)
     slots = exchange(terms, "dp")
     spots = slot_spots(got)
-    slots, spots = lax.optimization_barrier((slots, spots))
+    first_grad, second_grad = decoder_grads(got, spots, cols, lat_width)
+    slots, first_grad = lax.optimization_barrier((slots, first_grad))
     grads, part = slot_totals(slots, rank)
-    share = slots[:, 2 * tokens :, :]
+    share = slots[:, tokens:, :]
     (other,) = from_hops(share, "layer", layers, (2,))
     all_grads = exchange(grads, "dp")
-    first_grad, second_grad = decoder_grads(got, slots, spots, cols, lat_width)
     part = functools.reduce(jnp.add, from_hops(part, "layer", layers, (1, 2, 3)), part)
-    all_grads, first_grad, part = lax.optimization_barrier((all_grads, first_grad, part))
+    far = from_hops(part, "layer", layers, (4, 8, 12))
+    latent_grad = functools.reduce(jnp.add, far, part)
+    all_grads, latent_grad = lax.optimization_barrier((all_grads, latent_grad))
     encoder_grad = encoder_grads(own, share, other, spots, all_grads, cols, lat_width)
-    far = from_hops(part, "layer", layers, (4, 8, 12))
-    *far, encoder_grad = lax.optimization_barrier((*far, encoder_grad))
-    latent_grad = functools.reduce(jnp.add, far, part)
     return (
         first_grad.transpose(2, 0, 1),
         second_grad.T,

time: 130 us -> 138 us (1.062)
  waiting for transfers between devices: 41.2 us -> 47.6 us
  starting transfers between devices: 35.3 us -> 38.1 us
  Pallas kernels: 49.2 us -> 47.7 us
    ppermute x7, waiting for transfers between devices: 0.5 us -> 15.4 us  [from_hops(): lax.ppermute(array, axis, [(at, at ^ hop) for at in range(size)])]
    all_to_all x3, waiting for transfers between devices: 40.7 us -> 32.2 us  [exchange(): return lax.all_to_all(array, axis, 0, 0, tiled=True)]
    all_to_all x3, starting transfers between devices: 20.9 us -> 23.8 us  [exchange(): return lax.all_to_all(array, axis, 0, 0, tiled=True)]
    pallas_call x1 -> x0, Pallas kernels: 1.82 us -> none  [slot_values(): pl.pallas_call(values_kernel, out_shape=jax.ShapeDtypeStruct((value.shape...]
  transfers between devices with their start and end apart: 10 -> 10, of which waited for: 4 -> 5; matrix products, arithmetic and copies ran while one was open for 0% -> 0% of each run, Pallas kernels for 29% -> 18%
where the time goes in v1:
time: 138 us; the launch traced here: 136 us
  Pallas kernels  47.7 us (35%)
  waiting for transfers between devices  47.6 us (34%)
  starting transfers between devices  38.1 us (28%)
    all_to_all x3, waiting for transfers between devices, exchange(): return lax.all_to_all(array, axis, 0, 0, tiled=True)  32.2 us
    all_to_all x3, starting transfers between devices, exchange(): return lax.all_to_all(array, axis, 0, 0, tiled=True)  23.8 us
    ppermute x7, waiting for transfers between devices, from_hops(): lax.ppermute(array, axis, [(at, at ^ hop) for at in range(size)])  15.4 us
    ppermute x7, starting transfers between devices, from_hops(): lax.ppermute(array, axis, [(at, at ^ hop) for at in range(size)])  14.3 us
    pallas_call x1, Pallas kernels, encoder_grads(): pl.pallas_call(back_kernel, grid=(parts // shards,), in_specs=[pl.BlockSp...  10.3 us
    pallas_call x1, Pallas kernels, slot_spots(): pl.pallas_call(spots_kernel, grid=(parts // shards,), in_specs=[pl.BlockS...  10.1 us
    pallas_call x1, Pallas kernels, decoder_grads(): pl.pallas_call(codes_kernel, grid=(parts // shards,), in_specs=[pl.BlockS...  9.98 us
    pallas_call x1, Pallas kernels, slot_terms(): pl.pallas_call(terms_kernel, grid=(parts // shards,), in_specs=[pl.BlockS...  6.64 us
  transfers between devices with their start and end apart: 10, of which 5 were waited for; matrix products, arithmetic and copies ran while one was open for 0% of the time, Pallas kernels for 18%

profile of v1, /device:TPU:2, one launch (start us, length us, event | category | flops | bytes accessed | tf_op | source)
XLA Modules:
  0.0 136.2 jit_solution(9105436543131727340)
XLA Ops:
  0.7 0.6 pad_add_fusion.own_ref
  1.2 6.0 %shard_map.103 = (bf16[16,704,128]{2,1,0:T(8,128)(2,1)}, s32[2,64,128]{2,1,0:T(8,128)}) custom-call(s32[2]{0:T(128)} %pad_add_fusion.own_ref, bf16[2,128,3584]{2,1,0:T(8,128)(2,1)} %cot_ref.1, s32[2,64,128]{2,1,0:T(8,128)} %bitcast.12, bf16[2,64,128]{2,1,0:T(8,128)(2,1)} %bitcast.13, s32[2,128]{1,0:T(2,128)} %live_ref.1), custom_call_target="tpu_custom_call" | custom-call | bytes 5242880 | tf_op jit(solution)/shard_map/pallas_call | solution.py:90
  7.3 7.5 %all-to-all-start = ((bf16[16,704,128]{2,1,0:T(8,128)(2,1)}), bf16[16,704,128]{2,1,0:T(8,128)(2,1)}, u32[]{:S(2)}, u32[]{:S(2)}) async-start(bf16[16,704,128]{2,1,0:T(8,128)(2,1)} %get-tuple-element.14), calls=%async_computation | async-start | bytes 5767168 | tf_op jit(solution)/shard_map/all_to_all | solution.py:462
  14.7 4.2 %shard_map.102.half_ref = bf16[16,224,128]{2,1,0:T(8,128)(2,1)} custom-call(s32[2]{0:T(128)} %pad_add_fusion.own_ref, bf16[2,128,3584]{2,1,0:T(8,128)(2,1)} %res_ref.1), custom_call_target="tpu_custom_call" | custom-call | bytes 2097152 | tf_op jit(solution)/shard_map/pallas_call | solution.py:124
  19.0 32.0 %all-to-all-done.got_ref = bf16[16,704,128]{2,1,0:T(8,128)(2,1)} async-done(((bf16[16,704,128]{2,1,0:T(8,128)(2,1)}), bf16[16,704,128]{2,1,0:T(8,128)(2,1)}, u32[]{:S(2)}, u32[]{:S(2)}) %all-to-all-start) | async-done | bytes 2883616 | tf_op jit(solution)/shard_map/all_to_all | solution.py:462
  50.9 6.6 %shard_map.104 = bf16[16,352,128]{2,1,0:T(8,128)(2,1)} custom-call(bf16[2,224,512]{2,1,0:T(8,128)(2,1)} %bitcast.10, bf16[224,512]{1,0:T(8,128)(2,1)} %bitcast.11, bf16[16,224,128]{2,1,0:T(8,128)(2,1)} %shard_map.102.half_ref, bf16[16,704,128]{2,1,0:T(8,128)(2,1)} %all-to-all-done.got_ref), custom_call_target="tpu_custom_call" | custom-call | flops 1409286144 | bytes 6291456 | tf_op jit(solution)/shard_map/pallas_call | solution.py:174
  57.5 9.3 %all-to-all-start.1 = ((bf16[16,352,128]{2,1,0:T(8,128)(2,1)}), bf16[16,352,128]{2,1,0:T(8,128)(2,1)S(1)}, u32[]{:S(2)}, u32[]{:S(2)}) async-start(bf16[16,352,128]{2,1,0:T(8,128)(2,1)} %shard_map.104), calls=%async_computation.1 | async-start | bytes 2883584 | tf_op jit(solution)/shard_map/all_to_all | solution.py:462
  66.9 10.1 %shard_map.105.spot_ref = s32[16,256,128]{2,1,0:T(8,128)} custom-call(bf16[16,704,128]{2,1,0:T(8,128)(2,1)} %all-to-all-done.got_ref), custom_call_target="tpu_custom_call" | custom-call | flops 4294967296 | bytes 8388608 | tf_op jit(solution)/shard_map/pallas_call | solution.py:281
  77.0 10.0 %shard_map.106 = (bf16[2,224,512]{2,1,0:T(8,128)(2,1)}, bf16[224,512]{1,0:T(8,128)(2,1)}) custom-call(bf16[16,704,128]{2,1,0:T(8,128)(2,1)} %all-to-all-done.got_ref, s32[16,256,128]{2,1,0:T(8,128)} %shard_map.105.spot_ref), custom_call_target="tpu_custom_call" | custom-call | flops 1409286144 | bytes 8388608 | tf_op jit(solution)/shard_map/pallas_call | solution.py:380
  86.9 0.3 all-to-all-done.1.got_ref
  87.3 2.0 %collective-permute-start = (bf16[16,224,128]{2,1,0:T(8,128)(2,1)S(1)}, bf16[16,224,128]{2,1,0:T(8,128)(2,1)S(1)}, u32[]{:S(2)}, u32[]{:S(2)}) collective-permute-start(bf16[16,224,128]{2,1,0:T(8,128)(2,1)S(1)} %slice.3.mine_ref), channel_id=1, source_target_pairs={{0,32},{16,48},{32,0},{48,16},{64,96},{80,112},{96,64},{112,80},{1... | collective-permute-start | bytes 2752520 | tf_op jit(solution)/shard_map/ppermute | solution.py:466
  89.3 0.5 shard_map.107
  89.8 0.8 copy-done
  90.6 0.5 collective-permute-start.3
  91.1 1.6 %collective-permute-start.2 = (bf16[2,64,128]{2,1,0:T(8,128)(2,1)S(1)}, bf16[2,64,128]{2,1,0:T(8,128)(2,1)S(1)}, u32[]{:S(2)}, u32[]{:S(2)}) collective-permute-start(bf16[2,64,128]{2,1,0:T(8,128)(2,1)S(1)} %get-tuple-element.21), channel_id=1, source_target_pairs={{0,32},{16,48},{32,0},{48,16},{64,96},{80,112},{96,64},{112,80},{1... | collective-permute-start | bytes 98312 | tf_op jit(solution)/shard_map/ppermute | solution.py:466
  92.7 1.3 collective-permute-start.1
  94.0 7.0 %all-to-all-start.2 = ((bf16[16,128,128]{2,1,0:T(8,128)(2,1)}), bf16[16,128,128]{2,1,0:T(8,128)(2,1)S(1)}, u32[]{:S(2)}, u32[]{:S(2)}) async-start(bf16[16,128,128]{2,1,0:T(8,128)(2,1)} %copy-done), calls=%async_computation.2 | async-start | bytes 1048576 | tf_op jit(solution)/shard_map/all_to_all | solution.py:462
  101.0 9.8 %collective-permute-done.3 = bf16[2,64,128]{2,1,0:T(8,128)(2,1)S(1)} collective-permute-done((bf16[2,64,128]{2,1,0:T(8,128)(2,1)S(1)}, bf16[2,64,128]{2,1,0:T(8,128)(2,1)S(1)}, u32[]{:S(2)}, u32[]{:S(2)}) %collective-permute-start.3) | collective-permute-done | bytes 32800 | tf_op jit(solution)/shard_map/ppermute | solution.py:466
  111.1 6.2 %collective-permute-start.6 = (bf16[2,64,128]{2,1,0:T(8,128)(2,1)S(1)}, bf16[2,64,128]{2,1,0:T(8,128)(2,1)S(1)}, u32[]{:S(2)}, u32[]{:S(2)}) collective-permute-start(bf16[2,64,128]{2,1,0:T(8,128)(2,1)S(1)} %add_add_fusion.1), channel_id=1, source_target_pairs={{0,192},{16,208},{32,224},{48,240},{64,128},{80,144},{96,160},{112... | collective-permute-start | bytes 98312 | tf_op jit(solution)/shard_map/ppermute | solution.py:466
  117.3 1.2 collective-permute-start.5
  118.5 1.5 %collective-permute-start.4 = (bf16[2,64,128]{2,1,0:T(8,128)(2,1)S(1)}, bf16[2,64,128]{2,1,0:T(8,128)(2,1)S(1)}, u32[]{:S(2)}, u32[]{:S(2)}) collective-permute-start(bf16[2,64,128]{2,1,0:T(8,128)(2,1)S(1)} %add_add_fusion.1), channel_id=1, source_target_pairs={{0,64},{16,80},{32,96},{48,112},{64,0},{80,16},{96,32},{112,48},{1... | collective-permute-start | bytes 98312 | tf_op jit(solution)/shard_map/ppermute | solution.py:466
  120.0 5.3 %collective-permute-done.5 = bf16[2,64,128]{2,1,0:T(8,128)(2,1)S(1)} collective-permute-done((bf16[2,64,128]{2,1,0:T(8,128)(2,1)S(1)}, bf16[2,64,128]{2,1,0:T(8,128)(2,1)S(1)}, u32[]{:S(2)}, u32[]{:S(2)}) %collective-permute-start.5) | collective-permute-done | bytes 32800 | tf_op jit(solution)/shard_map/ppermute | solution.py:466
  125.3 0.6 convert_bitcast_fusion
  125.9 10.3 %shard_map.108 = bf16[224,2,512]{2,1,0:T(2,128)(2,1)} custom-call(s32[2]{0:T(128)S(1)} %copy-done.2, bf16[16,224,128]{2,1,0:T(8,128)(2,1)S(1)} %slice.3.mine_ref, bf16[16,224,128]{2,1,0:T(8,128)(2,1)S(1)} %collective-permute-done.other_ref, s32[16,256,128]{2,1,0:T(8,128)} %shard_map.105.spot_ref, bf16[16,128,128]{2,1,0:T(8,128)(2,1)S(1)} %all-to-all-done.2.grad_ref), custom_call_target="tpu_custom_call" | custom-call | flops 939524096 | bytes 8388608 | tf_op jit(solution)/shard_map/pallas_call | solution.py:440
  (14 shorter events, 0.3 us)
Async XLA Ops:
  7.3 43.6 %all-to-all-start = ((bf16[16,704,128]{2,1,0:T(8,128)(2,1)}), bf16[16,704,128]{2,1,0:T(8,128)(2,1)}, u32[]{:S(2)}, u32[]{:S(2)}) async-start(bf16[16,704,128]{2,1,0:T(8,128)(2,1)} %get-tuple-element.14), calls=%async_computation | async-start | bytes 5767168 | tf_op jit(solution)/shard_map/all_to_all | solution.py:462
  57.5 29.7 %all-to-all-start.1 = ((bf16[16,352,128]{2,1,0:T(8,128)(2,1)}), bf16[16,352,128]{2,1,0:T(8,128)(2,1)S(1)}, u32[]{:S(2)}, u32[]{:S(2)}) async-start(bf16[16,352,128]{2,1,0:T(8,128)(2,1)} %shard_map.104), calls=%async_computation.1 | async-start | bytes 2883584 | tf_op jit(solution)/shard_map/all_to_all | solution.py:462
  86.9 2.3 %copy-start.1 = (s32[2,64,128]{2,1,0:T(8,128)S(1)}, s32[2,64,128]{2,1,0:T(8,128)}, u32[]{:S(2)}) copy-start(s32[2,64,128]{2,1,0:T(8,128)} %get-tuple-element.19.rank_ref) | copy-start | bytes 196612
  87.3 38.6 %copy-start.2 = (s32[2]{0:T(128)S(1)}, s32[2]{0:T(128)}, u32[]{:S(2)}) copy-start(s32[2]{0:T(128)} %pad_add_fusion.own_ref) | copy-start | bytes 28
  87.3 38.6 %collective-permute-start = (bf16[16,224,128]{2,1,0:T(8,128)(2,1)S(1)}, bf16[16,224,128]{2,1,0:T(8,128)(2,1)S(1)}, u32[]{:S(2)}, u32[]{:S(2)}) collective-permute-start(bf16[16,224,128]{2,1,0:T(8,128)(2,1)S(1)} %slice.3.mine_ref), channel_id=1, source_target_pairs={{0,32},{16,48},{32,0},{48,16},{64,96},{80,112},{96,64},{112,80},{1... | collective-permute-start | bytes 2752520 | tf_op jit(solution)/shard_map/ppermute | solution.py:466
  89.8 0.8 copy-start
  90.6 20.3 %collective-permute-start.3 = (bf16[2,64,128]{2,1,0:T(8,128)(2,1)S(1)}, bf16[2,64,128]{2,1,0:T(8,128)(2,1)S(1)}, u32[]{:S(2)}, u32[]{:S(2)}) collective-permute-start(bf16[2,64,128]{2,1,0:T(8,128)(2,1)S(1)} %get-tuple-element.21), channel_id=1, source_target_pairs={{0,48},{16,32},{32,16},{48,0},{64,112},{80,96},{96,80},{112,64},{1... | collective-permute-start | bytes 98312 | tf_op jit(solution)/shard_map/ppermute | solution.py:466
  91.1 20.0 %collective-permute-start.2 = (bf16[2,64,128]{2,1,0:T(8,128)(2,1)S(1)}, bf16[2,64,128]{2,1,0:T(8,128)(2,1)S(1)}, u32[]{:S(2)}, u32[]{:S(2)}) collective-permute-start(bf16[2,64,128]{2,1,0:T(8,128)(2,1)S(1)} %get-tuple-element.21), channel_id=1, source_target_pairs={{0,32},{16,48},{32,0},{48,16},{64,96},{80,112},{96,64},{112,80},{1... | collective-permute-start | bytes 98312 | tf_op jit(solution)/shard_map/ppermute | solution.py:466
  92.7 18.4 %collective-permute-start.1 = (bf16[2,64,128]{2,1,0:T(8,128)(2,1)S(1)}, bf16[2,64,128]{2,1,0:T(8,128)(2,1)S(1)}, u32[]{:S(2)}, u32[]{:S(2)}) collective-permute-start(bf16[2,64,128]{2,1,0:T(8,128)(2,1)S(1)} %get-tuple-element.21), channel_id=1, source_target_pairs={{0,16},{16,0},{32,48},{48,32},{64,80},{80,64},{96,112},{112,96},{1... | collective-permute-start | bytes 98312 | tf_op jit(solution)/shard_map/ppermute | solution.py:466
  94.0 31.2 %all-to-all-start.2 = ((bf16[16,128,128]{2,1,0:T(8,128)(2,1)}), bf16[16,128,128]{2,1,0:T(8,128)(2,1)S(1)}, u32[]{:S(2)}, u32[]{:S(2)}) async-start(bf16[16,128,128]{2,1,0:T(8,128)(2,1)} %copy-done), calls=%async_computation.2 | async-start | bytes 1048576 | tf_op jit(solution)/shard_map/all_to_all | solution.py:462
  111.1 8.9 %collective-permute-start.6 = (bf16[2,64,128]{2,1,0:T(8,128)(2,1)S(1)}, bf16[2,64,128]{2,1,0:T(8,128)(2,1)S(1)}, u32[]{:S(2)}, u32[]{:S(2)}) collective-permute-start(bf16[2,64,128]{2,1,0:T(8,128)(2,1)S(1)} %add_add_fusion.1), channel_id=1, source_target_pairs={{0,192},{16,208},{32,224},{48,240},{64,128},{80,144},{96,160},{112... | collective-permute-start | bytes 98312 | tf_op jit(solution)/shard_map/ppermute | solution.py:466
  117.3 7.9 %collective-permute-start.5 = (bf16[2,64,128]{2,1,0:T(8,128)(2,1)S(1)}, bf16[2,64,128]{2,1,0:T(8,128)(2,1)S(1)}, u32[]{:S(2)}, u32[]{:S(2)}) collective-permute-start(bf16[2,64,128]{2,1,0:T(8,128)(2,1)S(1)} %add_add_fusion.1), channel_id=1, source_target_pairs={{0,128},{16,144},{32,160},{48,176},{64,192},{80,208},{96,224},{112... | collective-permute-start | bytes 98312 | tf_op jit(solution)/shard_map/ppermute | solution.py:466
  118.5 6.8 %collective-permute-start.4 = (bf16[2,64,128]{2,1,0:T(8,128)(2,1)S(1)}, bf16[2,64,128]{2,1,0:T(8,128)(2,1)S(1)}, u32[]{:S(2)}, u32[]{:S(2)}) collective-permute-start(bf16[2,64,128]{2,1,0:T(8,128)(2,1)S(1)} %add_add_fusion.1), channel_id=1, source_target_pairs={{0,64},{16,80},{32,96},{48,112},{64,0},{80,16},{96,32},{112,48},{1... | collective-permute-start | bytes 98312 | tf_op jit(solution)/shard_map/ppermute | solution.py:466

commit v2 on v1

--- a/solution.py
+++ b/solution.py
@@ -486,8 +486,8 @@
     share = slots[:, tokens:, :]
     (other,) = from_hops(share, "layer", layers, (2,))
     all_grads = exchange(grads, "dp")
-    part = functools.reduce(jnp.add, from_hops(part, "layer", layers, (1, 2, 3)), part)
-    far = from_hops(part, "layer", layers, (4, 8, 12))
+    part = functools.reduce(jnp.add, from_hops(part, "layer", layers, (1, 4, 5)), part)
+    far = from_hops(part, "layer", layers, (2, 8, 10))
     latent_grad = functools.reduce(jnp.add, far, part)
     all_grads, latent_grad = lax.optimization_barrier((all_grads, latent_grad))
     encoder_grad = encoder_grads(own, share, other, spots, all_grads, cols, lat_width)

time: 138 us -> 139 us (level)
  starting transfers between devices: 38.1 us -> 40.1 us
    ppermute x7, starting transfers between devices: 14.3 us -> 16.3 us  [from_hops(): lax.ppermute(array, axis, [(at, at ^ hop) for at in range(size)])]
  transfers between devices with their start and end apart: 10 -> 10, of which waited for: 5 -> 6; matrix products, arithmetic and copies ran while one was open for 0% -> 0% of each run, Pallas kernels for 18% -> 18%
where the time goes in v2:
time: 139 us; the launch traced here: 137 us
  Pallas kernels  47.7 us (34%)
  waiting for transfers between devices  46.4 us (33%)
  starting transfers between devices  40.1 us (29%)
    all_to_all x3, waiting for transfers between devices, exchange(): return lax.all_to_all(array, axis, 0, 0, tiled=True)  32.2 us
    all_to_all x3, starting transfers between devices, exchange(): return lax.all_to_all(array, axis, 0, 0, tiled=True)  23.8 us
    ppermute x7, starting transfers between devices, from_hops(): lax.ppermute(array, axis, [(at, at ^ hop) for at in range(size)])  16.3 us
    ppermute x7, waiting for transfers between devices, from_hops(): lax.ppermute(array, axis, [(at, at ^ hop) for at in range(size)])  14.2 us
    pallas_call x1, Pallas kernels, encoder_grads(): pl.pallas_call(back_kernel, grid=(parts // shards,), in_specs=[pl.BlockSp...  10.3 us
    pallas_call x1, Pallas kernels, slot_spots(): pl.pallas_call(spots_kernel, grid=(parts // shards,), in_specs=[pl.BlockS...  10.1 us
    pallas_call x1, Pallas kernels, decoder_grads(): pl.pallas_call(codes_kernel, grid=(parts // shards,), in_specs=[pl.BlockS...  9.98 us
    pallas_call x1, Pallas kernels, slot_terms(): pl.pallas_call(terms_kernel, grid=(parts // shards,), in_specs=[pl.BlockS...  6.64 us
  transfers between devices with their start and end apart: 10, of which 6 were waited for; matrix products, arithmetic and copies ran while one was open for 0% of the time, Pallas kernels for 18%

profile of v2, /device:TPU:2, one launch (start us, length us, event | category | flops | bytes accessed | tf_op | source)
XLA Modules:
  0.0 137.0 jit_solution(18395161227824638537)
XLA Ops:
  0.7 0.6 pad_add_fusion.own_ref
  1.2 6.0 %shard_map.103 = (bf16[16,704,128]{2,1,0:T(8,128)(2,1)}, s32[2,64,128]{2,1,0:T(8,128)}) custom-call(s32[2]{0:T(128)} %pad_add_fusion.own_ref, bf16[2,128,3584]{2,1,0:T(8,128)(2,1)} %cot_ref.1, s32[2,64,128]{2,1,0:T(8,128)} %bitcast.12, bf16[2,64,128]{2,1,0:T(8,128)(2,1)} %bitcast.13, s32[2,128]{1,0:T(2,128)} %live_ref.1), custom_call_target="tpu_custom_call" | custom-call | bytes 5242880 | tf_op jit(solution)/shard_map/pallas_call | solution.py:90
  7.3 7.5 %all-to-all-start = ((bf16[16,704,128]{2,1,0:T(8,128)(2,1)}), bf16[16,704,128]{2,1,0:T(8,128)(2,1)}, u32[]{:S(2)}, u32[]{:S(2)}) async-start(bf16[16,704,128]{2,1,0:T(8,128)(2,1)} %get-tuple-element.14), calls=%async_computation | async-start | bytes 5767168 | tf_op jit(solution)/shard_map/all_to_all | solution.py:462
  14.7 4.2 %shard_map.102.half_ref = bf16[16,224,128]{2,1,0:T(8,128)(2,1)} custom-call(s32[2]{0:T(128)} %pad_add_fusion.own_ref, bf16[2,128,3584]{2,1,0:T(8,128)(2,1)} %res_ref.1), custom_call_target="tpu_custom_call" | custom-call | bytes 2097152 | tf_op jit(solution)/shard_map/pallas_call | solution.py:124
  19.0 32.0 %all-to-all-done.got_ref = bf16[16,704,128]{2,1,0:T(8,128)(2,1)} async-done(((bf16[16,704,128]{2,1,0:T(8,128)(2,1)}), bf16[16,704,128]{2,1,0:T(8,128)(2,1)}, u32[]{:S(2)}, u32[]{:S(2)}) %all-to-all-start) | async-done | bytes 2883616 | tf_op jit(solution)/shard_map/all_to_all | solution.py:462
  50.9 6.6 %shard_map.104 = bf16[16,352,128]{2,1,0:T(8,128)(2,1)} custom-call(bf16[2,224,512]{2,1,0:T(8,128)(2,1)} %bitcast.10, bf16[224,512]{1,0:T(8,128)(2,1)} %bitcast.11, bf16[16,224,128]{2,1,0:T(8,128)(2,1)} %shard_map.102.half_ref, bf16[16,704,128]{2,1,0:T(8,128)(2,1)} %all-to-all-done.got_ref), custom_call_target="tpu_custom_call" | custom-call | flops 1409286144 | bytes 6291456 | tf_op jit(solution)/shard_map/pallas_call | solution.py:174
  57.5 9.3 %all-to-all-start.1 = ((bf16[16,352,128]{2,1,0:T(8,128)(2,1)}), bf16[16,352,128]{2,1,0:T(8,128)(2,1)S(1)}, u32[]{:S(2)}, u32[]{:S(2)}) async-start(bf16[16,352,128]{2,1,0:T(8,128)(2,1)} %shard_map.104), calls=%async_computation.1 | async-start | bytes 2883584 | tf_op jit(solution)/shard_map/all_to_all | solution.py:462
  66.9 10.1 %shard_map.105.spot_ref = s32[16,256,128]{2,1,0:T(8,128)} custom-call(bf16[16,704,128]{2,1,0:T(8,128)(2,1)} %all-to-all-done.got_ref), custom_call_target="tpu_custom_call" | custom-call | flops 4294967296 | bytes 8388608 | tf_op jit(solution)/shard_map/pallas_call | solution.py:281
  77.0 10.0 %shard_map.106 = (bf16[2,224,512]{2,1,0:T(8,128)(2,1)}, bf16[224,512]{1,0:T(8,128)(2,1)}) custom-call(bf16[16,704,128]{2,1,0:T(8,128)(2,1)} %all-to-all-done.got_ref, s32[16,256,128]{2,1,0:T(8,128)} %shard_map.105.spot_ref), custom_call_target="tpu_custom_call" | custom-call | flops 1409286144 | bytes 8388608 | tf_op jit(solution)/shard_map/pallas_call | solution.py:380
  86.9 0.3 all-to-all-done.1.got_ref
  87.3 2.0 %collective-permute-start = (bf16[16,224,128]{2,1,0:T(8,128)(2,1)S(1)}, bf16[16,224,128]{2,1,0:T(8,128)(2,1)S(1)}, u32[]{:S(2)}, u32[]{:S(2)}) collective-permute-start(bf16[16,224,128]{2,1,0:T(8,128)(2,1)S(1)} %slice.3.mine_ref), channel_id=1, source_target_pairs={{0,32},{16,48},{32,0},{48,16},{64,96},{80,112},{96,64},{112,80},{1... | collective-permute-start | bytes 2752520 | tf_op jit(solution)/shard_map/ppermute | solution.py:466
  89.3 0.5 shard_map.107
  89.8 0.8 copy-done
  90.6 3.4 %collective-permute-start.3 = (bf16[2,64,128]{2,1,0:T(8,128)(2,1)S(1)}, bf16[2,64,128]{2,1,0:T(8,128)(2,1)S(1)}, u32[]{:S(2)}, u32[]{:S(2)}) collective-permute-start(bf16[2,64,128]{2,1,0:T(8,128)(2,1)S(1)} %get-tuple-element.21), channel_id=1, source_target_pairs={{0,80},{16,64},{32,112},{48,96},{64,16},{80,0},{96,48},{112,32},{1... | collective-permute-start | bytes 98312 | tf_op jit(solution)/shard_map/ppermute | solution.py:466
  93.9 1.3 collective-permute-start.1
  95.3 7.0 %all-to-all-start.2 = ((bf16[16,128,128]{2,1,0:T(8,128)(2,1)}), bf16[16,128,128]{2,1,0:T(8,128)(2,1)S(1)}, u32[]{:S(2)}, u32[]{:S(2)}) async-start(bf16[16,128,128]{2,1,0:T(8,128)(2,1)} %copy-done), calls=%async_computation.2 | async-start | bytes 1048576 | tf_op jit(solution)/shard_map/all_to_all | solution.py:462
  102.3 7.7 %collective-permute-done.3 = bf16[2,64,128]{2,1,0:T(8,128)(2,1)S(1)} collective-permute-done((bf16[2,64,128]{2,1,0:T(8,128)(2,1)S(1)}, bf16[2,64,128]{2,1,0:T(8,128)(2,1)S(1)}, u32[]{:S(2)}, u32[]{:S(2)}) %collective-permute-start.3) | collective-permute-done | bytes 32800 | tf_op jit(solution)/shard_map/ppermute | solution.py:466
  110.0 0.4 collective-permute-done.2
  110.4 7.8 %collective-permute-start.6 = (bf16[2,64,128]{2,1,0:T(8,128)(2,1)S(1)}, bf16[2,64,128]{2,1,0:T(8,128)(2,1)S(1)}, u32[]{:S(2)}, u32[]{:S(2)}) collective-permute-start(bf16[2,64,128]{2,1,0:T(8,128)(2,1)S(1)} %add_add_fusion.1), channel_id=1, source_target_pairs={{0,160},{16,176},{32,128},{48,144},{64,224},{80,240},{96,192},{112... | collective-permute-start | bytes 98312 | tf_op jit(solution)/shard_map/ppermute | solution.py:466
  118.2 0.7 collective-permute-start.5
  118.9 1.0 collective-permute-start.4
  120.1 5.9 %collective-permute-done.5 = bf16[2,64,128]{2,1,0:T(8,128)(2,1)S(1)} collective-permute-done((bf16[2,64,128]{2,1,0:T(8,128)(2,1)S(1)}, bf16[2,64,128]{2,1,0:T(8,128)(2,1)S(1)}, u32[]{:S(2)}, u32[]{:S(2)}) %collective-permute-start.5) | collective-permute-done | bytes 32800 | tf_op jit(solution)/shard_map/ppermute | solution.py:466
  126.1 0.6 convert_bitcast_fusion
  126.7 10.3 %shard_map.108 = bf16[224,2,512]{2,1,0:T(2,128)(2,1)} custom-call(s32[2]{0:T(128)S(1)} %copy-done.2, bf16[16,224,128]{2,1,0:T(8,128)(2,1)S(1)} %slice.3.mine_ref, bf16[16,224,128]{2,1,0:T(8,128)(2,1)S(1)} %collective-permute-done.other_ref, s32[16,256,128]{2,1,0:T(8,128)} %shard_map.105.spot_ref, bf16[16,128,128]{2,1,0:T(8,128)(2,1)S(1)} %all-to-all-done.2.grad_ref), custom_call_target="tpu_custom_call" | custom-call | flops 939524096 | bytes 8388608 | tf_op jit(solution)/shard_map/pallas_call | solution.py:440
  (14 shorter events, 0.3 us)
Async XLA Ops:
  7.3 43.6 %all-to-all-start = ((bf16[16,704,128]{2,1,0:T(8,128)(2,1)}), bf16[16,704,128]{2,1,0:T(8,128)(2,1)}, u32[]{:S(2)}, u32[]{:S(2)}) async-start(bf16[16,704,128]{2,1,0:T(8,128)(2,1)} %get-tuple-element.14), calls=%async_computation | async-start | bytes 5767168 | tf_op jit(solution)/shard_map/all_to_all | solution.py:462
  57.5 29.7 %all-to-all-start.1 = ((bf16[16,352,128]{2,1,0:T(8,128)(2,1)}), bf16[16,352,128]{2,1,0:T(8,128)(2,1)S(1)}, u32[]{:S(2)}, u32[]{:S(2)}) async-start(bf16[16,352,128]{2,1,0:T(8,128)(2,1)} %shard_map.104), calls=%async_computation.1 | async-start | bytes 2883584 | tf_op jit(solution)/shard_map/all_to_all | solution.py:462
  86.9 2.3 %copy-start.1 = (s32[2,64,128]{2,1,0:T(8,128)S(1)}, s32[2,64,128]{2,1,0:T(8,128)}, u32[]{:S(2)}) copy-start(s32[2,64,128]{2,1,0:T(8,128)} %get-tuple-element.19.rank_ref) | copy-start | bytes 196612
  87.3 39.5 %copy-start.2 = (s32[2]{0:T(128)S(1)}, s32[2]{0:T(128)}, u32[]{:S(2)}) copy-start(s32[2]{0:T(128)} %pad_add_fusion.own_ref) | copy-start | bytes 28
  87.3 39.4 %collective-permute-start = (bf16[16,224,128]{2,1,0:T(8,128)(2,1)S(1)}, bf16[16,224,128]{2,1,0:T(8,128)(2,1)S(1)}, u32[]{:S(2)}, u32[]{:S(2)}) collective-permute-start(bf16[16,224,128]{2,1,0:T(8,128)(2,1)S(1)} %slice.3.mine_ref), channel_id=1, source_target_pairs={{0,32},{16,48},{32,0},{48,16},{64,96},{80,112},{96,64},{112,80},{1... | collective-permute-start | bytes 2752520 | tf_op jit(solution)/shard_map/ppermute | solution.py:466
  89.8 0.8 copy-start
  90.6 19.4 %collective-permute-start.3 = (bf16[2,64,128]{2,1,0:T(8,128)(2,1)S(1)}, bf16[2,64,128]{2,1,0:T(8,128)(2,1)S(1)}, u32[]{:S(2)}, u32[]{:S(2)}) collective-permute-start(bf16[2,64,128]{2,1,0:T(8,128)(2,1)S(1)} %get-tuple-element.21), channel_id=1, source_target_pairs={{0,80},{16,64},{32,112},{48,96},{64,16},{80,0},{96,48},{112,32},{1... | collective-permute-start | bytes 98312 | tf_op jit(solution)/shard_map/ppermute | solution.py:466
  93.9 16.4 %collective-permute-start.2 = (bf16[2,64,128]{2,1,0:T(8,128)(2,1)S(1)}, bf16[2,64,128]{2,1,0:T(8,128)(2,1)S(1)}, u32[]{:S(2)}, u32[]{:S(2)}) collective-permute-start(bf16[2,64,128]{2,1,0:T(8,128)(2,1)S(1)} %get-tuple-element.21), channel_id=1, source_target_pairs={{0,64},{16,80},{32,96},{48,112},{64,0},{80,16},{96,32},{112,48},{1... | collective-permute-start | bytes 98312 | tf_op jit(solution)/shard_map/ppermute | solution.py:466
  93.9 16.4 %collective-permute-start.1 = (bf16[2,64,128]{2,1,0:T(8,128)(2,1)S(1)}, bf16[2,64,128]{2,1,0:T(8,128)(2,1)S(1)}, u32[]{:S(2)}, u32[]{:S(2)}) collective-permute-start(bf16[2,64,128]{2,1,0:T(8,128)(2,1)S(1)} %get-tuple-element.21), channel_id=1, source_target_pairs={{0,16},{16,0},{32,48},{48,32},{64,80},{80,64},{96,112},{112,96},{1... | collective-permute-start | bytes 98312 | tf_op jit(solution)/shard_map/ppermute | solution.py:466
  95.3 30.8 %all-to-all-start.2 = ((bf16[16,128,128]{2,1,0:T(8,128)(2,1)}), bf16[16,128,128]{2,1,0:T(8,128)(2,1)S(1)}, u32[]{:S(2)}, u32[]{:S(2)}) async-start(bf16[16,128,128]{2,1,0:T(8,128)(2,1)} %copy-done), calls=%async_computation.2 | async-start | bytes 1048576 | tf_op jit(solution)/shard_map/all_to_all | solution.py:462
  110.4 9.7 %collective-permute-start.6 = (bf16[2,64,128]{2,1,0:T(8,128)(2,1)S(1)}, bf16[2,64,128]{2,1,0:T(8,128)(2,1)S(1)}, u32[]{:S(2)}, u32[]{:S(2)}) collective-permute-start(bf16[2,64,128]{2,1,0:T(8,128)(2,1)S(1)} %add_add_fusion.1), channel_id=1, source_target_pairs={{0,160},{16,176},{32,128},{48,144},{64,224},{80,240},{96,192},{112... | collective-permute-start | bytes 98312 | tf_op jit(solution)/shard_map/ppermute | solution.py:466
  118.2 7.8 %collective-permute-start.5 = (bf16[2,64,128]{2,1,0:T(8,128)(2,1)S(1)}, bf16[2,64,128]{2,1,0:T(8,128)(2,1)S(1)}, u32[]{:S(2)}, u32[]{:S(2)}) collective-permute-start(bf16[2,64,128]{2,1,0:T(8,128)(2,1)S(1)} %add_add_fusion.1), channel_id=1, source_target_pairs={{0,128},{16,144},{32,160},{48,176},{64,192},{80,208},{96,224},{112... | collective-permute-start | bytes 98312 | tf_op jit(solution)/shard_map/ppermute | solution.py:466
  118.9 7.1 %collective-permute-start.4 = (bf16[2,64,128]{2,1,0:T(8,128)(2,1)S(1)}, bf16[2,64,128]{2,1,0:T(8,128)(2,1)S(1)}, u32[]{:S(2)}, u32[]{:S(2)}) collective-permute-start(bf16[2,64,128]{2,1,0:T(8,128)(2,1)S(1)} %add_add_fusion.1), channel_id=1, source_target_pairs={{0,32},{16,48},{32,0},{48,16},{64,96},{80,112},{96,64},{112,80},{1... | collective-permute-start | bytes 98312 | tf_op jit(solution)/shard_map/ppermute | solution.py:466

commit v3 on v0

--- a/solution.py
+++ b/solution.py
@@ -41,7 +41,7 @@
 def kept_slots(own_ref, idx_ref, live_ref, layer, lat_width):
     slots, tokens = idx_ref.shape[1:]
     place = lax.broadcasted_iota(jnp.int32, (slots, tokens), 0)
-    local = idx_ref[layer] - own_ref[0]
+    local = idx_ref[layer] - own_ref[0] * lat_width
     inside = (place < live_ref[layer : layer + 1, :]) & (local >= 0) & (local < lat_width)
     return place, local, inside
 
@@ -106,8 +106,13 @@
     )(start, cotangent, index, live)
 
 
+def half_of(own):
+    return (own[0] >> 1) & 1
+
+
 def half_kernel(own_ref, res_ref, out_ref):
-    turn(jnp.concatenate([res_ref[own_ref[1]], res_ref[1 - own_ref[1]]], axis=0), out_ref, 0)
+    side = half_of(own_ref)
+    turn(jnp.concatenate([res_ref[side], res_ref[1 - side]], axis=0), out_ref, 0)
 
 
 def pack_half(parts, own, residual):
@@ -119,7 +124,7 @@
         grid_spec=pltpu.PrefetchScalarGridSpec(
             num_scalar_prefetch=1,
             grid=(steps,),
-            in_specs=[pl.BlockSpec((2, share, width // steps), lambda i, own: (0, own[1], i))],
+            in_specs=[pl.BlockSpec((2, share, width // steps), lambda i, own: (0, half_of(own), i))],
             out_specs=pl.BlockSpec((parts // steps, width // parts, tokens), lambda i, own: (i, 0, 0)),
         ),
         out_shape=jax.ShapeDtypeStruct((parts, width // parts, tokens), BF16),
@@ -429,7 +434,7 @@
         sum_ref[...] = jnp.zeros_like(sum_ref)
 
     lane = lax.broadcasted_iota(jnp.int32, (cols, tokens), 1)
-    mine = (lane < RUNS) == (own_ref[1] == 0)
+    mine = (lane < RUNS) == (half_of(own_ref) == 0)
 
     def product(first):
         rows = slice(first * tokens, (first + 2) * tokens)
@@ -489,9 +494,8 @@
     lat_width = decoder_first.shape[0]
     cols = decoder_second.shape[1]
     tokens = residual.shape[1]
-    members = 2
     place = lax.axis_index("layer")
-    own = jnp.stack([place * lat_width, place // 2 % members]).astype(jnp.int32)
+    own = place.astype(jnp.int32).reshape(1)
     index, value = latent_index.transpose(0, 2, 1), latent_value.transpose(0, 2, 1)
     packed, rank = pack(lat_width, parts, own, cotangent, index, active_count)
     got = exchange(packed, "dp")
@@ -506,10 +510,10 @@
     (other,) = from_hops(share, "layer", layers, (2,))
     all_grads = exchange(grads, "dp")
     first_grad, second_grad = decoder_grads(got, slots, spots, cols, lat_width)
-    part = functools.reduce(jnp.add, from_hops(part, "layer", layers, (1, 2, 3)), part)
+    part = functools.reduce(jnp.add, from_hops(part, "layer", layers, (4, 8, 12)), part)
     all_grads, first_grad, part = lax.optimization_barrier((all_grads, first_grad, part))
     encoder_grad = encoder_grads(own, share, other, spots, all_grads, cols, lat_width)
-    far = from_hops(part, "layer", layers, (4, 8, 12))
+    far = from_hops(part, "layer", layers, (1, 2, 3))
     *far, encoder_grad = lax.optimization_barrier((*far, encoder_grad))
     latent_grad = functools.reduce(jnp.add, far, part)
     return (

time: 130 us -> 130 us (level)
  waiting for transfers between devices: 41.2 us -> 44.3 us
  Pallas kernels: 49.2 us -> 47.8 us
    ppermute x7, waiting for transfers between devices: 0.5 us -> 2.94 us  [from_hops(): lax.ppermute(array, axis, [(at, at ^ hop) for at in range(size)])]
  transfers between devices with their start and end apart: 10 -> 10, of which waited for: 4 -> 4; matrix products, arithmetic and copies ran while one was open for 0% -> 0% of each run, Pallas kernels for 29% -> 28%
where the time goes in v3:
time: 130 us; the launch traced here: 129 us
  Pallas kernels  47.8 us (37%)
  waiting for transfers between devices  44.3 us (34%)
  starting transfers between devices  34.3 us (26%)
    all_to_all x3, waiting for transfers between devices, exchange(): return lax.all_to_all(array, axis, 0, 0, tiled=True)  41.4 us
    all_to_all x3, starting transfers between devices, exchange(): return lax.all_to_all(array, axis, 0, 0, tiled=True)  20.9 us
    ppermute x7, starting transfers between devices, from_hops(): lax.ppermute(array, axis, [(at, at ^ hop) for at in range(size)])  13.4 us
    pallas_call x1, Pallas kernels, encoder_grads(): pl.pallas_call(back_kernel, grid=(parts // shards,), in_specs=[pl.BlockSp...  10.4 us
    pallas_call x1, Pallas kernels, slot_spots(): pl.pallas_call(spots_kernel, grid=(parts // shards,), in_specs=[pl.BlockS...  10 us
    pallas_call x1, Pallas kernels, decoder_grads(): pl.pallas_call(codes_kernel, grid=(parts // shards,), in_specs=[pl.BlockS...  9.97 us
    pallas_call x1, Pallas kernels, slot_terms(): pl.pallas_call(terms_kernel, grid=(parts // shards,), in_specs=[pl.BlockS...  6.68 us
    pallas_call x1, Pallas kernels, pack(): pl.pallas_call(functools.partial(pack_kernel, lat_width), grid_spec=pltpu...  4.93 us
  transfers between devices with their start and end apart: 10, of which 4 were waited for; matrix products, arithmetic and copies ran while one was open for 0% of the time, Pallas kernels for 28%

profile of v3, /device:TPU:2, one launch (start us, length us, event | category | flops | bytes accessed | tf_op | source)
XLA Modules:
  0.0 128.6 jit_solution(8793213653559665564)
XLA Ops:
  0.6 4.9 %shard_map.102 = (bf16[16,576,128]{2,1,0:T(8,128)(2,1)}, s32[2,64,128]{2,1,0:T(8,128)}) custom-call(s32[1]{0:T(128)} %bitcast.2.own_ref, bf16[2,128,3584]{2,1,0:T(8,128)(2,1)} %cot_ref.1, s32[2,64,128]{2,1,0:T(8,128)} %bitcast.11, s32[2,128]{1,0:T(2,128)} %live_ref.1), custom_call_target="tpu_custom_call" | custom-call | bytes 5242880 | tf_op jit(solution)/shard_map/pallas_call | solution.py:84
  5.6 7.5 %all-to-all-start = ((bf16[16,576,128]{2,1,0:T(8,128)(2,1)}), bf16[16,576,128]{2,1,0:T(8,128)(2,1)}, u32[]{:S(2)}, u32[]{:S(2)}) async-start(bf16[16,576,128]{2,1,0:T(8,128)(2,1)} %get-tuple-element.20), calls=%async_computation | async-start | bytes 4718592 | tf_op jit(solution)/shard_map/all_to_all | solution.py:486
  13.0 3.5 %shard_map.104.half_ref = bf16[16,224,128]{2,1,0:T(8,128)(2,1)} custom-call(s32[1]{0:T(128)} %bitcast.2.own_ref, bf16[2,128,3584]{2,1,0:T(8,128)(2,1)} %res_ref.1), custom_call_target="tpu_custom_call" | custom-call | bytes 2097152 | tf_op jit(solution)/shard_map/pallas_call | solution.py:122
  16.6 1.8 %shard_map.103.val_ref = bf16[128,128]{1,0:T(8,128)(2,1)} custom-call(s32[2,64,128]{2,1,0:T(8,128)} %get-tuple-element.19.rank_ref, bf16[2,64,128]{2,1,0:T(8,128)(2,1)} %bitcast.12), custom_call_target="tpu_custom_call" | custom-call | bytes 1048576 | tf_op jit(solution)/shard_map/pallas_call | solution.py:151
  18.4 25.2 %all-to-all-done.got_ref = bf16[16,576,128]{2,1,0:T(8,128)(2,1)} async-done(((bf16[16,576,128]{2,1,0:T(8,128)(2,1)}), bf16[16,576,128]{2,1,0:T(8,128)(2,1)}, u32[]{:S(2)}, u32[]{:S(2)}) %all-to-all-start) | async-done | bytes 2359328 | tf_op jit(solution)/shard_map/all_to_all | solution.py:486
  43.6 6.7 %shard_map.105 = bf16[16,480,128]{2,1,0:T(8,128)(2,1)} custom-call(bf16[2,224,512]{2,1,0:T(8,128)(2,1)} %bitcast.9, bf16[224,512]{1,0:T(8,128)(2,1)} %bitcast.10, bf16[128,128]{1,0:T(8,128)(2,1)} %shard_map.103.val_ref, bf16[16,224,128]{2,1,0:T(8,128)(2,1)} %shard_map.104.half_ref, bf16[16,576,128]{2,1,0:T(8,128)(2,1)} %all-to-all-done.got_ref), custom_call_target="tpu_custom_call" | custom-call | flops 1409286144 | bytes 6291456 | tf_op jit(solution)/shard_map/pallas_call | solution.py:196
  50.3 7.2 %all-to-all-start.1 = ((bf16[16,480,128]{2,1,0:T(8,128)(2,1)}), bf16[16,480,128]{2,1,0:T(8,128)(2,1)S(1)}, u32[]{:S(2)}, u32[]{:S(2)}) async-start(bf16[16,480,128]{2,1,0:T(8,128)(2,1)} %shard_map.105), calls=%async_computation.1 | async-start | bytes 3932160 | tf_op jit(solution)/shard_map/all_to_all | solution.py:486
  57.5 10.0 %shard_map.106.spot_ref = s32[16,256,128]{2,1,0:T(8,128)} custom-call(bf16[16,576,128]{2,1,0:T(8,128)(2,1)} %all-to-all-done.got_ref), custom_call_target="tpu_custom_call" | custom-call | flops 4294967296 | bytes 8388608 | tf_op jit(solution)/shard_map/pallas_call | solution.py:304
  67.5 16.2 %all-to-all-done.1.got_ref.val_ref = bf16[16,480,128]{2,1,0:T(8,128)(2,1)S(1)} async-done(((bf16[16,480,128]{2,1,0:T(8,128)(2,1)}), bf16[16,480,128]{2,1,0:T(8,128)(2,1)S(1)}, u32[]{:S(2)}, u32[]{:S(2)}) %all-to-all-start.1) | async-done | bytes 1966112 | tf_op jit(solution)/shard_map/all_to_all | solution.py:486
  83.7 2.0 %collective-permute-start.6 = (bf16[16,224,128]{2,1,0:T(8,128)(2,1)S(1)}, bf16[16,224,128]{2,1,0:T(8,128)(2,1)}, u32[]{:S(2)}, u32[]{:S(2)}) collective-permute-start(bf16[16,224,128]{2,1,0:T(8,128)(2,1)S(1)} %slice.3.mine_ref), channel_id=1, source_target_pairs={{0,32},{16,48},{32,0},{48,16},{64,96},{80,112},{96,64},{112,80},{1... | collective-permute-start | bytes 2752520 | tf_op jit(solution)/shard_map/ppermute | solution.py:490
  85.7 0.5 shard_map.107
  86.2 0.8 copy-done
  87.0 6.2 %all-to-all-start.2 = ((bf16[16,128,128]{2,1,0:T(8,128)(2,1)}), bf16[16,128,128]{2,1,0:T(8,128)(2,1)S(1)}, u32[]{:S(2)}, u32[]{:S(2)}) async-start(bf16[16,128,128]{2,1,0:T(8,128)(2,1)} %copy-done), calls=%async_computation.2 | async-start | bytes 1048576 | tf_op jit(solution)/shard_map/all_to_all | solution.py:486
  93.2 5.4 %collective-permute-start.2 = (bf16[2,64,128]{2,1,0:T(8,128)(2,1)S(1)}, bf16[2,64,128]{2,1,0:T(8,128)(2,1)S(1)}, u32[]{:S(2)}, u32[]{:S(2)}) collective-permute-start(bf16[2,64,128]{2,1,0:T(8,128)(2,1)S(1)} %get-tuple-element.25), channel_id=1, source_target_pairs={{0,192},{16,208},{32,224},{48,240},{64,128},{80,144},{96,160},{112... | collective-permute-start | bytes 98312 | tf_op jit(solution)/shard_map/ppermute | solution.py:490
  98.6 1.4 %collective-permute-start.1 = (bf16[2,64,128]{2,1,0:T(8,128)(2,1)S(1)}, bf16[2,64,128]{2,1,0:T(8,128)(2,1)S(1)}, u32[]{:S(2)}, u32[]{:S(2)}) collective-permute-start(bf16[2,64,128]{2,1,0:T(8,128)(2,1)S(1)} %get-tuple-element.25), channel_id=1, source_target_pairs={{0,128},{16,144},{32,160},{48,176},{64,192},{80,208},{96,224},{112... | collective-permute-start | bytes 98312 | tf_op jit(solution)/shard_map/ppermute | solution.py:490
  100.1 1.0 collective-permute-start
  101.1 10.0 %shard_map.108 = (bf16[2,224,512]{2,1,0:T(8,128)(2,1)}, bf16[224,512]{1,0:T(8,128)(2,1)}) custom-call(bf16[16,576,128]{2,1,0:T(8,128)(2,1)} %all-to-all-done.got_ref, bf16[16,480,128]{2,1,0:T(8,128)(2,1)S(1)} %all-to-all-done.1.got_ref.val_ref, s32[16,256,128]{2,1,0:T(8,128)} %shard_map.106.spot_ref), custom_call_target="tpu_custom_call" | custom-call | flops 1409286144 | bytes 8388608 | tf_op jit(solution)/shard_map/pallas_call | solution.py:403
  111.1 2.0 %collective-permute-done.2 = bf16[2,64,128]{2,1,0:T(8,128)(2,1)S(1)} collective-permute-done((bf16[2,64,128]{2,1,0:T(8,128)(2,1)S(1)}, bf16[2,64,128]{2,1,0:T(8,128)(2,1)S(1)}, u32[]{:S(2)}, u32[]{:S(2)}) %collective-permute-start.2) | collective-permute-done | bytes 32800 | tf_op jit(solution)/shard_map/ppermute | solution.py:490
  113.1 0.9 collective-permute-done.1
  114.0 1.6 %collective-permute-start.5 = (bf16[2,64,128]{2,1,0:T(8,128)(2,1)S(1)}, bf16[2,64,128]{2,1,0:T(8,128)(2,1)S(1)}, u32[]{:S(2)}, u32[]{:S(2)}) collective-permute-start(bf16[2,64,128]{2,1,0:T(8,128)(2,1)S(1)} %add_add_fusion), channel_id=1, source_target_pairs={{0,48},{16,32},{32,16},{48,0},{64,112},{80,96},{96,80},{112,64},{1... | collective-permute-start | bytes 98312 | tf_op jit(solution)/shard_map/ppermute | solution.py:490
  115.6 0.7 collective-permute-start.4
  116.2 1.3 %collective-permute-start.3 = (bf16[2,64,128]{2,1,0:T(8,128)(2,1)S(1)}, bf16[2,64,128]{2,1,0:T(8,128)(2,1)S(1)}, u32[]{:S(2)}, u32[]{:S(2)}) collective-permute-start(bf16[2,64,128]{2,1,0:T(8,128)(2,1)S(1)} %add_add_fusion), channel_id=1, source_target_pairs={{0,16},{16,0},{32,48},{48,32},{64,80},{80,64},{96,112},{112,96},{1... | collective-permute-start | bytes 98312 | tf_op jit(solution)/shard_map/ppermute | solution.py:490
  117.6 10.4 %shard_map.109 = bf16[224,2,512]{2,1,0:T(2,128)(2,1)} custom-call(s32[1]{0:T(128)} %bitcast.2.own_ref, bf16[16,224,128]{2,1,0:T(8,128)(2,1)S(1)} %slice.3.mine_ref, bf16[16,224,128]{2,1,0:T(8,128)(2,1)} %collective-permute-done.6.other_ref, s32[16,256,128]{2,1,0:T(8,128)} %shard_map.106.spot_ref, bf16[16,128,128]{2,1,0:T(8,128)(2,1)S(1)} %all-to-all-done.2.grad_ref), custom_call_target="tpu_custom_call" | custom-call | flops 939524096 | bytes 8388608 | tf_op jit(solution)/shard_map/pallas_call | solution.py:464
  128.0 0.6 convert_bitcast_fusion
  (11 shorter events, 0.1 us)
Async XLA Ops:
  5.6 38.0 %all-to-all-start = ((bf16[16,576,128]{2,1,0:T(8,128)(2,1)}), bf16[16,576,128]{2,1,0:T(8,128)(2,1)}, u32[]{:S(2)}, u32[]{:S(2)}) async-start(bf16[16,576,128]{2,1,0:T(8,128)(2,1)} %get-tuple-element.20), calls=%async_computation | async-start | bytes 4718592 | tf_op jit(solution)/shard_map/all_to_all | solution.py:486
  50.3 33.4 %all-to-all-start.1 = ((bf16[16,480,128]{2,1,0:T(8,128)(2,1)}), bf16[16,480,128]{2,1,0:T(8,128)(2,1)S(1)}, u32[]{:S(2)}, u32[]{:S(2)}) async-start(bf16[16,480,128]{2,1,0:T(8,128)(2,1)} %shard_map.105), calls=%async_computation.1 | async-start | bytes 3932160 | tf_op jit(solution)/shard_map/all_to_all | solution.py:486
  57.5 28.3 %copy-start.1 = (s32[2,64,128]{2,1,0:T(8,128)S(1)}, s32[2,64,128]{2,1,0:T(8,128)}, u32[]{:S(2)}) copy-start(s32[2,64,128]{2,1,0:T(8,128)} %get-tuple-element.19.rank_ref) | copy-start | bytes 196612
  83.7 33.9 %collective-permute-start.6 = (bf16[16,224,128]{2,1,0:T(8,128)(2,1)S(1)}, bf16[16,224,128]{2,1,0:T(8,128)(2,1)}, u32[]{:S(2)}, u32[]{:S(2)}) collective-permute-start(bf16[16,224,128]{2,1,0:T(8,128)(2,1)S(1)} %slice.3.mine_ref), channel_id=1, source_target_pairs={{0,32},{16,48},{32,0},{48,16},{64,96},{80,112},{96,64},{112,80},{1... | collective-permute-start | bytes 2752520 | tf_op jit(solution)/shard_map/ppermute | solution.py:490
  86.2 0.8 copy-start
  87.0 27.0 %all-to-all-start.2 = ((bf16[16,128,128]{2,1,0:T(8,128)(2,1)}), bf16[16,128,128]{2,1,0:T(8,128)(2,1)S(1)}, u32[]{:S(2)}, u32[]{:S(2)}) async-start(bf16[16,128,128]{2,1,0:T(8,128)(2,1)} %copy-done), calls=%async_computation.2 | async-start | bytes 1048576 | tf_op jit(solution)/shard_map/all_to_all | solution.py:486
  93.2 19.9 %collective-permute-start.2 = (bf16[2,64,128]{2,1,0:T(8,128)(2,1)S(1)}, bf16[2,64,128]{2,1,0:T(8,128)(2,1)S(1)}, u32[]{:S(2)}, u32[]{:S(2)}) collective-permute-start(bf16[2,64,128]{2,1,0:T(8,128)(2,1)S(1)} %get-tuple-element.25), channel_id=1, source_target_pairs={{0,192},{16,208},{32,224},{48,240},{64,128},{80,144},{96,160},{112... | collective-permute-start | bytes 98312 | tf_op jit(solution)/shard_map/ppermute | solution.py:490
  98.6 15.4 %collective-permute-start.1 = (bf16[2,64,128]{2,1,0:T(8,128)(2,1)S(1)}, bf16[2,64,128]{2,1,0:T(8,128)(2,1)S(1)}, u32[]{:S(2)}, u32[]{:S(2)}) collective-permute-start(bf16[2,64,128]{2,1,0:T(8,128)(2,1)S(1)} %get-tuple-element.25), channel_id=1, source_target_pairs={{0,128},{16,144},{32,160},{48,176},{64,192},{80,208},{96,224},{112... | collective-permute-start | bytes 98312 | tf_op jit(solution)/shard_map/ppermute | solution.py:490
  100.1 13.9 %collective-permute-start = (bf16[2,64,128]{2,1,0:T(8,128)(2,1)S(1)}, bf16[2,64,128]{2,1,0:T(8,128)(2,1)S(1)}, u32[]{:S(2)}, u32[]{:S(2)}) collective-permute-start(bf16[2,64,128]{2,1,0:T(8,128)(2,1)S(1)} %get-tuple-element.25), channel_id=1, source_target_pairs={{0,64},{16,80},{32,96},{48,112},{64,0},{80,16},{96,32},{112,48},{1... | collective-permute-start | bytes 98312 | tf_op jit(solution)/shard_map/ppermute | solution.py:490
  114.0 13.9 %collective-permute-start.5 = (bf16[2,64,128]{2,1,0:T(8,128)(2,1)S(1)}, bf16[2,64,128]{2,1,0:T(8,128)(2,1)S(1)}, u32[]{:S(2)}, u32[]{:S(2)}) collective-permute-start(bf16[2,64,128]{2,1,0:T(8,128)(2,1)S(1)} %add_add_fusion), channel_id=1, source_target_pairs={{0,48},{16,32},{32,16},{48,0},{64,112},{80,96},{96,80},{112,64},{1... | collective-permute-start | bytes 98312 | tf_op jit(solution)/shard_map/ppermute | solution.py:490
  115.6 12.4 %collective-permute-start.4 = (bf16[2,64,128]{2,1,0:T(8,128)(2,1)S(1)}, bf16[2,64,128]{2,1,0:T(8,128)(2,1)S(1)}, u32[]{:S(2)}, u32[]{:S(2)}) collective-permute-start(bf16[2,64,128]{2,1,0:T(8,128)(2,1)S(1)} %add_add_fusion), channel_id=1, source_target_pairs={{0,32},{16,48},{32,0},{48,16},{64,96},{80,112},{96,64},{112,80},{1... | collective-permute-start | bytes 98312 | tf_op jit(solution)/shard_map/ppermute | solution.py:490
  116.2 11.7 %collective-permute-start.3 = (bf16[2,64,128]{2,1,0:T(8,128)(2,1)S(1)}, bf16[2,64,128]{2,1,0:T(8,128)(2,1)S(1)}, u32[]{:S(2)}, u32[]{:S(2)}) collective-permute-start(bf16[2,64,128]{2,1,0:T(8,128)(2,1)S(1)} %add_add_fusion), channel_id=1, source_target_pairs={{0,16},{16,0},{32,48},{48,32},{64,80},{80,64},{96,112},{112,96},{1... | collective-permute-start | bytes 98312 | tf_op jit(solution)/shard_map/ppermute | solution.py:490

commit v4 on v3

--- a/solution.py
+++ b/solution.py
@@ -162,17 +162,16 @@
 
     @pl.when(pl.program_id(0) == 0)
     def _():
-        weight_ref[0:cols, 0:lat_width] = wf_ref[0]
-        weight_ref[cols : 2 * cols, 0:lat_width] = wf_ref[1]
-        weight_ref[0:cols, lat_width:] = jnp.zeros((cols, lat_width), BF16)
-        weight_ref[cols : 2 * cols, lat_width:] = ws_ref[...]
+        weight_ref[0:cols, :] = wf_ref[0]
+        weight_ref[cols : 2 * cols, :] = wf_ref[1]
 
     out_ref[:, 2 * tokens :, :] = half_ref[...]
     pair = 2
     for first in range(0, shards, pair):
         some = range(first, first + pair)
         cot = jnp.concatenate([got_ref[shard, 0 : 2 * cols, :] for shard in some], axis=1)
-        dense = jnp.dot(cot.T, weight_ref[...], preferred_element_type=F32)
+        dot = functools.partial(jnp.dot, preferred_element_type=F32)
+        dense = (dot(cot.T, weight_ref[...]), dot(cot[cols:].T, ws_ref[...]))
         held = jnp.concatenate([got_ref[shard, 2 * cols :, :] for shard in some], axis=0)
         held = held.astype(F32).astype(jnp.int32) + SHIFT
         lane = lax.broadcasted_iota(jnp.int32, held.shape, 1)
@@ -182,7 +181,7 @@
         within = jnp.where((held & 1) == 1, RUNS, 0) + (held >> 3)
         picked = jnp.zeros(held.shape, F32)
         for part in range(2 * chunks):
-            table = dense[:, part * LANES : (part + 1) * LANES]
+            table = dense[part // chunks][:, part % chunks * LANES : (part % chunks + 1) * LANES]
             picked = jnp.where(chunk == part, lane_pick(table, within), picked)
         for shard in some:
             out_ref[shard, 0:tokens, :] = picked[(shard - first) * tokens : (shard - first + 1) * tokens].astype(BF16)
@@ -205,7 +204,7 @@
         ],
         out_specs=pl.BlockSpec((shards, 2 * tokens + cols, LANES), lambda i: (i, 0, 0)),
         out_shape=jax.ShapeDtypeStruct((parts, 2 * tokens + cols, LANES), BF16),
-        scratch_shapes=[pltpu.VMEM((2 * cols, 2 * lat_width), BF16)],
+        scratch_shapes=[pltpu.VMEM((2 * cols, lat_width), BF16)],
         compiler_params=grant(TERMS_MIB),
         cost_estimate=cost(2 * parts * tokens * cols * 3 * lat_width, 6 << 20),
     )(first, second, values, half, got)
@@ -510,10 +509,10 @@
     (other,) = from_hops(share, "layer", layers, (2,))
     all_grads = exchange(grads, "dp")
     first_grad, second_grad = decoder_grads(got, slots, spots, cols, lat_width)
-    part = functools.reduce(jnp.add, from_hops(part, "layer", layers, (4, 8, 12)), part)
+    part = functools.reduce(jnp.add, from_hops(part, "layer", layers, (1, 2, 3)), part)
     all_grads, first_grad, part = lax.optimization_barrier((all_grads, first_grad, part))
     encoder_grad = encoder_grads(own, share, other, spots, all_grads, cols, lat_width)
-    far = from_hops(part, "layer", layers, (1, 2, 3))
+    far = from_hops(part, "layer", layers, (4, 8, 12))
     *far, encoder_grad = lax.optimization_barrier((*far, encoder_grad))
     latent_grad = functools.reduce(jnp.add, far, part)
     return (

time: 130 us -> 129 us (level)
  waiting for transfers between devices: 44.3 us -> 42 us
  starting transfers between devices: 34.3 us -> 35.6 us
    ppermute x7, waiting for transfers between devices: 2.94 us -> 0.6 us  [from_hops(): lax.ppermute(array, axis, [(at, at ^ hop) for at in range(size)])]
where the time goes in v4:
time: 129 us; the launch traced here: 128 us
  Pallas kernels  47.9 us (37%)
  waiting for transfers between devices  42 us (33%)
  starting transfers between devices  35.6 us (28%)
    all_to_all x3, waiting for transfers between devices, exchange(): return lax.all_to_all(array, axis, 0, 0, tiled=True)  41.4 us
    all_to_all x3, starting transfers between devices, exchange(): return lax.all_to_all(array, axis, 0, 0, tiled=True)  20.9 us
    ppermute x7, starting transfers between devices, from_hops(): lax.ppermute(array, axis, [(at, at ^ hop) for at in range(size)])  14.7 us
    pallas_call x1, Pallas kernels, encoder_grads(): pl.pallas_call(back_kernel, grid=(parts // shards,), in_specs=[pl.BlockSp...  10.4 us
    pallas_call x1, Pallas kernels, slot_spots(): pl.pallas_call(spots_kernel, grid=(parts // shards,), in_specs=[pl.BlockS...  10 us
    pallas_call x1, Pallas kernels, decoder_grads(): pl.pallas_call(codes_kernel, grid=(parts // shards,), in_specs=[pl.BlockS...  9.97 us
    pallas_call x1, Pallas kernels, slot_terms(): pl.pallas_call(terms_kernel, grid=(parts // shards,), in_specs=[pl.BlockS...  6.8 us
    pallas_call x1, Pallas kernels, pack(): pl.pallas_call(functools.partial(pack_kernel, lat_width), grid_spec=pltpu...  4.93 us
  transfers between devices with their start and end apart: 10, of which 4 were waited for; matrix products, arithmetic and copies ran while one was open for 0% of the time, Pallas kernels for 28%

profile of v4, /device:TPU:2, one launch (start us, length us, event | category | flops | bytes accessed | tf_op | source)
XLA Modules:
  0.0 127.6 jit_solution(12737482316635545717)
XLA Ops:
  0.6 4.9 %shard_map.102 = (bf16[16,576,128]{2,1,0:T(8,128)(2,1)}, s32[2,64,128]{2,1,0:T(8,128)}) custom-call(s32[1]{0:T(128)} %bitcast.2.own_ref, bf16[2,128,3584]{2,1,0:T(8,128)(2,1)} %cot_ref.1, s32[2,64,128]{2,1,0:T(8,128)} %bitcast.11, s32[2,128]{1,0:T(2,128)} %live_ref.1), custom_call_target="tpu_custom_call" | custom-call | bytes 5242880 | tf_op jit(solution)/shard_map/pallas_call | solution.py:84
  5.6 7.5 %all-to-all-start = ((bf16[16,576,128]{2,1,0:T(8,128)(2,1)}), bf16[16,576,128]{2,1,0:T(8,128)(2,1)}, u32[]{:S(2)}, u32[]{:S(2)}) async-start(bf16[16,576,128]{2,1,0:T(8,128)(2,1)} %get-tuple-element.20), calls=%async_computation | async-start | bytes 4718592 | tf_op jit(solution)/shard_map/all_to_all | solution.py:485
  13.0 3.5 %shard_map.104.half_ref = bf16[16,224,128]{2,1,0:T(8,128)(2,1)} custom-call(s32[1]{0:T(128)} %bitcast.2.own_ref, bf16[2,128,3584]{2,1,0:T(8,128)(2,1)} %res_ref.1), custom_call_target="tpu_custom_call" | custom-call | bytes 2097152 | tf_op jit(solution)/shard_map/pallas_call | solution.py:122
  16.6 1.8 %shard_map.103.val_ref = bf16[128,128]{1,0:T(8,128)(2,1)} custom-call(s32[2,64,128]{2,1,0:T(8,128)} %get-tuple-element.19.rank_ref, bf16[2,64,128]{2,1,0:T(8,128)(2,1)} %bitcast.12), custom_call_target="tpu_custom_call" | custom-call | bytes 1048576 | tf_op jit(solution)/shard_map/pallas_call | solution.py:151
  18.4 25.2 %all-to-all-done.got_ref = bf16[16,576,128]{2,1,0:T(8,128)(2,1)} async-done(((bf16[16,576,128]{2,1,0:T(8,128)(2,1)}), bf16[16,576,128]{2,1,0:T(8,128)(2,1)}, u32[]{:S(2)}, u32[]{:S(2)}) %all-to-all-start) | async-done | bytes 2359328 | tf_op jit(solution)/shard_map/all_to_all | solution.py:485
  43.6 6.8 %shard_map.105 = bf16[16,480,128]{2,1,0:T(8,128)(2,1)} custom-call(bf16[2,224,512]{2,1,0:T(8,128)(2,1)} %bitcast.9, bf16[224,512]{1,0:T(8,128)(2,1)} %bitcast.10, bf16[128,128]{1,0:T(8,128)(2,1)} %shard_map.103.val_ref, bf16[16,224,128]{2,1,0:T(8,128)(2,1)} %shard_map.104.half_ref, bf16[16,576,128]{2,1,0:T(8,128)(2,1)} %all-to-all-done.got_ref), custom_call_target="tpu_custom_call" | custom-call | flops 1409286144 | bytes 6291456 | tf_op jit(solution)/shard_map/pallas_call | solution.py:195
  50.4 7.2 %all-to-all-start.1 = ((bf16[16,480,128]{2,1,0:T(8,128)(2,1)}), bf16[16,480,128]{2,1,0:T(8,128)(2,1)S(1)}, u32[]{:S(2)}, u32[]{:S(2)}) async-start(bf16[16,480,128]{2,1,0:T(8,128)(2,1)} %shard_map.105), calls=%async_computation.1 | async-start | bytes 3932160 | tf_op jit(solution)/shard_map/all_to_all | solution.py:485
  57.6 10.0 %shard_map.106.spot_ref = s32[16,256,128]{2,1,0:T(8,128)} custom-call(bf16[16,576,128]{2,1,0:T(8,128)(2,1)} %all-to-all-done.got_ref), custom_call_target="tpu_custom_call" | custom-call | flops 4294967296 | bytes 8388608 | tf_op jit(solution)/shard_map/pallas_call | solution.py:303
  67.6 16.2 %all-to-all-done.1.got_ref.val_ref = bf16[16,480,128]{2,1,0:T(8,128)(2,1)S(1)} async-done(((bf16[16,480,128]{2,1,0:T(8,128)(2,1)}), bf16[16,480,128]{2,1,0:T(8,128)(2,1)S(1)}, u32[]{:S(2)}, u32[]{:S(2)}) %all-to-all-start.1) | async-done | bytes 1966112 | tf_op jit(solution)/shard_map/all_to_all | solution.py:485
  83.8 2.0 %collective-permute-start.6 = (bf16[16,224,128]{2,1,0:T(8,128)(2,1)S(1)}, bf16[16,224,128]{2,1,0:T(8,128)(2,1)}, u32[]{:S(2)}, u32[]{:S(2)}) collective-permute-start(bf16[16,224,128]{2,1,0:T(8,128)(2,1)S(1)} %slice.3.mine_ref), channel_id=1, source_target_pairs={{0,32},{16,48},{32,0},{48,16},{64,96},{80,112},{96,64},{112,80},{1... | collective-permute-start | bytes 2752520 | tf_op jit(solution)/shard_map/ppermute | solution.py:489
  85.8 0.5 shard_map.107
  86.3 0.8 copy-done
  87.1 6.2 %all-to-all-start.2 = ((bf16[16,128,128]{2,1,0:T(8,128)(2,1)}), bf16[16,128,128]{2,1,0:T(8,128)(2,1)S(1)}, u32[]{:S(2)}, u32[]{:S(2)}) async-start(bf16[16,128,128]{2,1,0:T(8,128)(2,1)} %copy-done), calls=%async_computation.2 | async-start | bytes 1048576 | tf_op jit(solution)/shard_map/all_to_all | solution.py:485
  93.3 0.2 collective-permute-start.2
  93.6 1.9 %collective-permute-start.1 = (bf16[2,64,128]{2,1,0:T(8,128)(2,1)S(1)}, bf16[2,64,128]{2,1,0:T(8,128)(2,1)S(1)}, u32[]{:S(2)}, u32[]{:S(2)}) collective-permute-start(bf16[2,64,128]{2,1,0:T(8,128)(2,1)S(1)} %get-tuple-element.25), channel_id=1, source_target_pairs={{0,32},{16,48},{32,0},{48,16},{64,96},{80,112},{96,64},{112,80},{1... | collective-permute-start | bytes 98312 | tf_op jit(solution)/shard_map/ppermute | solution.py:489
  95.5 1.3 %collective-permute-start = (bf16[2,64,128]{2,1,0:T(8,128)(2,1)S(1)}, bf16[2,64,128]{2,1,0:T(8,128)(2,1)S(1)}, u32[]{:S(2)}, u32[]{:S(2)}) collective-permute-start(bf16[2,64,128]{2,1,0:T(8,128)(2,1)S(1)} %get-tuple-element.25), channel_id=1, source_target_pairs={{0,16},{16,0},{32,48},{48,32},{64,80},{80,64},{96,112},{112,96},{1... | collective-permute-start | bytes 98312 | tf_op jit(solution)/shard_map/ppermute | solution.py:489
  96.8 10.0 %shard_map.108 = (bf16[2,224,512]{2,1,0:T(8,128)(2,1)}, bf16[224,512]{1,0:T(8,128)(2,1)}) custom-call(bf16[16,576,128]{2,1,0:T(8,128)(2,1)} %all-to-all-done.got_ref, bf16[16,480,128]{2,1,0:T(8,128)(2,1)S(1)} %all-to-all-done.1.got_ref.val_ref, s32[16,256,128]{2,1,0:T(8,128)} %shard_map.106.spot_ref), custom_call_target="tpu_custom_call" | custom-call | flops 1409286144 | bytes 8388608 | tf_op jit(solution)/shard_map/pallas_call | solution.py:402
  106.8 0.4 collective-permute-done.2
  107.2 0.2 collective-permute-done.1
  107.4 6.2 %collective-permute-start.5 = (bf16[2,64,128]{2,1,0:T(8,128)(2,1)S(1)}, bf16[2,64,128]{2,1,0:T(8,128)(2,1)S(1)}, u32[]{:S(2)}, u32[]{:S(2)}) collective-permute-start(bf16[2,64,128]{2,1,0:T(8,128)(2,1)S(1)} %add_add_fusion), channel_id=1, source_target_pairs={{0,192},{16,208},{32,224},{48,240},{64,128},{80,144},{96,160},{112... | collective-permute-start | bytes 98312 | tf_op jit(solution)/shard_map/ppermute | solution.py:489
  113.6 2.7 %collective-permute-start.4 = (bf16[2,64,128]{2,1,0:T(8,128)(2,1)S(1)}, bf16[2,64,128]{2,1,0:T(8,128)(2,1)S(1)}, u32[]{:S(2)}, u32[]{:S(2)}) collective-permute-start(bf16[2,64,128]{2,1,0:T(8,128)(2,1)S(1)} %add_add_fusion), channel_id=1, source_target_pairs={{0,128},{16,144},{32,160},{48,176},{64,192},{80,208},{96,224},{112... | collective-permute-start | bytes 98312 | tf_op jit(solution)/shard_map/ppermute | solution.py:489
  116.3 0.3 collective-permute-start.3
  116.6 10.4 %shard_map.109 = bf16[224,2,512]{2,1,0:T(2,128)(2,1)} custom-call(s32[1]{0:T(128)} %bitcast.2.own_ref, bf16[16,224,128]{2,1,0:T(8,128)(2,1)S(1)} %slice.3.mine_ref, bf16[16,224,128]{2,1,0:T(8,128)(2,1)} %collective-permute-done.6.other_ref, s32[16,256,128]{2,1,0:T(8,128)} %shard_map.106.spot_ref, bf16[16,128,128]{2,1,0:T(8,128)(2,1)S(1)} %all-to-all-done.2.grad_ref), custom_call_target="tpu_custom_call" | custom-call | flops 939524096 | bytes 8388608 | tf_op jit(solution)/shard_map/pallas_call | solution.py:463
  127.0 0.6 convert_bitcast_fusion
  (11 shorter events, 0.1 us)
Async XLA Ops:
  5.6 38.0 %all-to-all-start = ((bf16[16,576,128]{2,1,0:T(8,128)(2,1)}), bf16[16,576,128]{2,1,0:T(8,128)(2,1)}, u32[]{:S(2)}, u32[]{:S(2)}) async-start(bf16[16,576,128]{2,1,0:T(8,128)(2,1)} %get-tuple-element.20), calls=%async_computation | async-start | bytes 4718592 | tf_op jit(solution)/shard_map/all_to_all | solution.py:485
  50.4 33.4 %all-to-all-start.1 = ((bf16[16,480,128]{2,1,0:T(8,128)(2,1)}), bf16[16,480,128]{2,1,0:T(8,128)(2,1)S(1)}, u32[]{:S(2)}, u32[]{:S(2)}) async-start(bf16[16,480,128]{2,1,0:T(8,128)(2,1)} %shard_map.105), calls=%async_computation.1 | async-start | bytes 3932160 | tf_op jit(solution)/shard_map/all_to_all | solution.py:485
  57.6 28.3 %copy-start.1 = (s32[2,64,128]{2,1,0:T(8,128)S(1)}, s32[2,64,128]{2,1,0:T(8,128)}, u32[]{:S(2)}) copy-start(s32[2,64,128]{2,1,0:T(8,128)} %get-tuple-element.19.rank_ref) | copy-start | bytes 196612
  83.8 32.8 %collective-permute-start.6 = (bf16[16,224,128]{2,1,0:T(8,128)(2,1)S(1)}, bf16[16,224,128]{2,1,0:T(8,128)(2,1)}, u32[]{:S(2)}, u32[]{:S(2)}) collective-permute-start(bf16[16,224,128]{2,1,0:T(8,128)(2,1)S(1)} %slice.3.mine_ref), channel_id=1, source_target_pairs={{0,32},{16,48},{32,0},{48,16},{64,96},{80,112},{96,64},{112,80},{1... | collective-permute-start | bytes 2752520 | tf_op jit(solution)/shard_map/ppermute | solution.py:489
  86.3 0.8 copy-start
  87.1 20.3 %all-to-all-start.2 = ((bf16[16,128,128]{2,1,0:T(8,128)(2,1)}), bf16[16,128,128]{2,1,0:T(8,128)(2,1)S(1)}, u32[]{:S(2)}, u32[]{:S(2)}) async-start(bf16[16,128,128]{2,1,0:T(8,128)(2,1)} %copy-done), calls=%async_computation.2 | async-start | bytes 1048576 | tf_op jit(solution)/shard_map/all_to_all | solution.py:485
  93.3 13.8 %collective-permute-start.2 = (bf16[2,64,128]{2,1,0:T(8,128)(2,1)S(1)}, bf16[2,64,128]{2,1,0:T(8,128)(2,1)S(1)}, u32[]{:S(2)}, u32[]{:S(2)}) collective-permute-start(bf16[2,64,128]{2,1,0:T(8,128)(2,1)S(1)} %get-tuple-element.25), channel_id=1, source_target_pairs={{0,48},{16,32},{32,16},{48,0},{64,112},{80,96},{96,80},{112,64},{1... | collective-permute-start | bytes 98312 | tf_op jit(solution)/shard_map/ppermute | solution.py:489
  93.6 13.8 %collective-permute-start.1 = (bf16[2,64,128]{2,1,0:T(8,128)(2,1)S(1)}, bf16[2,64,128]{2,1,0:T(8,128)(2,1)S(1)}, u32[]{:S(2)}, u32[]{:S(2)}) collective-permute-start(bf16[2,64,128]{2,1,0:T(8,128)(2,1)S(1)} %get-tuple-element.25), channel_id=1, source_target_pairs={{0,32},{16,48},{32,0},{48,16},{64,96},{80,112},{96,64},{112,80},{1... | collective-permute-start | bytes 98312 | tf_op jit(solution)/shard_map/ppermute | solution.py:489
  95.5 11.9 %collective-permute-start = (bf16[2,64,128]{2,1,0:T(8,128)(2,1)S(1)}, bf16[2,64,128]{2,1,0:T(8,128)(2,1)S(1)}, u32[]{:S(2)}, u32[]{:S(2)}) collective-permute-start(bf16[2,64,128]{2,1,0:T(8,128)(2,1)S(1)} %get-tuple-element.25), channel_id=1, source_target_pairs={{0,16},{16,0},{32,48},{48,32},{64,80},{80,64},{96,112},{112,96},{1... | collective-permute-start | bytes 98312 | tf_op jit(solution)/shard_map/ppermute | solution.py:489
  107.4 19.6 %collective-permute-start.5 = (bf16[2,64,128]{2,1,0:T(8,128)(2,1)S(1)}, bf16[2,64,128]{2,1,0:T(8,128)(2,1)S(1)}, u32[]{:S(2)}, u32[]{:S(2)}) collective-permute-start(bf16[2,64,128]{2,1,0:T(8,128)(2,1)S(1)} %add_add_fusion), channel_id=1, source_target_pairs={{0,192},{16,208},{32,224},{48,240},{64,128},{80,144},{96,160},{112... | collective-permute-start | bytes 98312 | tf_op jit(solution)/shard_map/ppermute | solution.py:489
  113.6 13.3 %collective-permute-start.4 = (bf16[2,64,128]{2,1,0:T(8,128)(2,1)S(1)}, bf16[2,64,128]{2,1,0:T(8,128)(2,1)S(1)}, u32[]{:S(2)}, u32[]{:S(2)}) collective-permute-start(bf16[2,64,128]{2,1,0:T(8,128)(2,1)S(1)} %add_add_fusion), channel_id=1, source_target_pairs={{0,128},{16,144},{32,160},{48,176},{64,192},{80,208},{96,224},{112... | collective-permute-start | bytes 98312 | tf_op jit(solution)/shard_map/ppermute | solution.py:489
  116.3 10.7 %collective-permute-start.3 = (bf16[2,64,128]{2,1,0:T(8,128)(2,1)S(1)}, bf16[2,64,128]{2,1,0:T(8,128)(2,1)S(1)}, u32[]{:S(2)}, u32[]{:S(2)}) collective-permute-start(bf16[2,64,128]{2,1,0:T(8,128)(2,1)S(1)} %add_add_fusion), channel_id=1, source_target_pairs={{0,64},{16,80},{32,96},{48,112},{64,0},{80,16},{96,32},{112,48},{1... | collective-permute-start | bytes 98312 | tf_op jit(solution)/shard_map/ppermute | solution.py:489
